TPU v7x, 32 devices: a whole 2x2x4 slice. The times are simulated.
32 devices in a mesh: dev: 32 (over z, y, x, core).
Axes of the slice: x: 2, y: 2, z: 4, core: 2. Of those that a mesh axis runs over, the one named last changes fastest.
Arguments:
- embeddings: bfloat16 [8192, 1024], P('dev'), may hold values from -6 to 6
- cluster_id: int32 [8192], P('dev'), may hold values from 0 to 15, as said below
- requests: int32 [1024], P('dev'), may hold values from -1 to 1, as said below
- pair_left: int32 [12288], P('dev'), may hold values from 0 to 31, as said below
- pair_right: int32 [12288], P('dev'), may hold values from 0 to 31, as said below
Outputs:
- best: float32 [8192], P('dev')
Inputs may be any that keep to these rules, and one draw needn't show every extreme that they name: Rows are sorted by cluster: cluster_id never falls along the rows, and every cluster has rows. Every slot that some task of device d names has a block (requests at least 0 there); a device's tasks name slots of at most 32 consecutive owners. pair_left <= pair_right for every task; no device lists one slot pair twice. `pair_right`: see pair_left.
All inputs are finite; a program needn't handle non-finite values.
Results may differ from a plain program's by a relative error of at most 0.00086.
Values may be sent and summed in bfloat16 or wider, within the bound.
No kernel may reach another device: no remote copies, remote signals or barrier semaphores. Data moves between devices by JAX's collectives and lax.ppermute only.
A program may use at most 192 MiB of HBM per device.

v0:
```python
import jax
import jax.numpy as jnp
from jax import lax
from jax.sharding import PartitionSpec as P

D = 1024
BLOCK = 128
GROUP = 64


def local(embeddings, cluster_id, requests, pair_left, pair_right):
    devices = lax.axis_size("dev")
    blk_dev = embeddings.shape[0] // BLOCK
    values = embeddings.astype(jnp.float32)
    unit = (values * lax.rsqrt(jnp.sum(values * values, axis=-1, keepdims=True) + 1e-06)).astype(
        jnp.bfloat16
    )
    unit = unit.reshape(blk_dev, BLOCK, D)
    labels = cluster_id.reshape(blk_dev, BLOCK)
    asked = lax.all_to_all(requests, "dev", split_axis=0, concat_axis=0, tiled=True)
    picked = jnp.clip(asked, 0, blk_dev - 1)
    outgoing = unit[picked]
    out_labels = labels[picked].astype(jnp.bfloat16)
    fetched, fetched_labels = (
        lax.all_to_all(outgoing, "dev", split_axis=0, concat_axis=0, tiled=True),
        lax.all_to_all(out_labels, "dev", split_axis=0, concat_axis=0, tiled=True),
    )
    fetched_labels = fetched_labels.astype(jnp.int32)
    diagonal_mask = jnp.eye(BLOCK, dtype=bool)

    def step(carry, indices):
        left, right = indices
        sims = jnp.einsum(
            "gid,gjd->gij", fetched[left], fetched[right], preferred_element_type=jnp.float32
        )
        same = fetched_labels[left][:, :, None] == fetched_labels[right][:, None, :]
        selfish = (left == right)[:, None, None] & diagonal_mask[None]
        sims = jnp.where(same & ~selfish, sims, jnp.float32(-1.0))
        carry = carry.at[left].max(jnp.max(sims, axis=2))
        carry = carry.at[right].max(jnp.max(sims, axis=1))
        return (carry, None)

    start = jnp.full((devices, BLOCK), -1.0, jnp.float32)
    slot_best, _ = lax.scan(
        step, start, (pair_left.reshape(-1, GROUP), pair_right.reshape(-1, GROUP))
    )
    returned = lax.all_to_all(slot_best, "dev", split_axis=0, concat_axis=0, tiled=True)
    masked = jnp.where((asked >= 0)[:, None], returned, jnp.float32(-1.0))
    result = jnp.full((blk_dev, BLOCK), -1.0, jnp.float32).at[picked].max(masked)
    return result.reshape(-1)


def solution(mesh):
    in_specs = (P("dev", None), P("dev"), P("dev"), P("dev"), P("dev"))
    out_specs = P("dev")
    return jax.shard_map(local, mesh=mesh, in_specs=in_specs, out_specs=out_specs, check_vma=False)
```

profile of v0, /device:TPU:0, one launch (start us, length us, event | category | flops | bytes accessed | tf_op | source)
XLA Modules:
  0.0 474.1 jit_solution(1648889390719897703)
XLA Ops:
  1.3 7.3 %all-to-all-start = ((s32[32,1,1]{2,1,0:T(1,128)}), s32[32,1,1]{2,1,0:T(1,128)S(1)}, u32[]{:S(2)}, u32[]{:S(2)}) async-start(s32[32,1,1]{2,1,0:T(1,128)} %copy.8), calls=%async_computation | async-start | bytes 32768 | tf_op jit(solution)/shard_map/all_to_all | solution.py:20
  9.9 5.9 %all-to-all-done = s32[32,1,1]{2,1,0:T(1,128)S(1)} async-done(((s32[32,1,1]{2,1,0:T(1,128)}), s32[32,1,1]{2,1,0:T(1,128)S(1)}, u32[]{:S(2)}, u32[]{:S(2)}) %all-to-all-start) | async-done | bytes 160 | tf_op jit(solution)/shard_map/all_to_all | solution.py:20
  18.2 2.5 all-to-all-start.1
  21.9 4.9 %gather_fusion.5 = bf16[32,128,1024]{2,1,0:T(8,128)(2,1)} fusion(bf16[2,128,1024]{2,1,0:T(8,128)(2,1)S(1)} %bitcast.37, s32[1024]{0:T(1024)S(1)} %pad_clamp_fusion.2), kind=kCustom, calls=%fused_computation.5 | custom fusion | bytes 16777344 | tf_op jit(solution)/shard_map/gather | solution.py:22
  27.8 4.9 %all-to-all-start.2 = ((bf16[32,128,1024]{2,1,0:T(8,128)(2,1)}), bf16[32,128,1024]{2,1,0:T(8,128)(2,1)}, u32[]{:S(2)}, u32[]{:S(2)}) async-start(bf16[32,128,1024]{2,1,0:T(8,128)(2,1)} %gather_fusion.5), calls=%async_computation.2 | async-start | bytes 16777216 | tf_op jit(solution)/shard_map/all_to_all | solution.py:25
  33.0 185.9 %all-to-all-done.2 = bf16[32,128,1024]{2,1,0:T(8,128)(2,1)} async-done(((bf16[32,128,1024]{2,1,0:T(8,128)(2,1)}), bf16[32,128,1024]{2,1,0:T(8,128)(2,1)}, u32[]{:S(2)}, u32[]{:S(2)}) %all-to-all-start.2) | async-done | bytes 8388640 | tf_op jit(solution)/shard_map/all_to_all | solution.py:25
  219.4 243.5 %while.11 = (s32[]{:T(128)}, f32[32,128]{1,0:T(8,128)}, s32[6,64]{1,0:T(8,128)S(1)}, s32[32,128]{1,0:T(8,128)S(1)}, s32[6,64]{1,0:T(8,128)S(1)}, /*index=5*/bf16[32,128,1024]{2,1,0:T(8,128)(2,1)}, s32[]{:T(128)}) while((s32[]{:T(128)}, f32[32,128]{1,0:T(8,128)}, s32[6,64]{1,0:T(8,128)S(1)}, s32[32,128]{1,0:T(8,128)S(1)}, ...), condition=%wide.region_6.7_spmd.clone, body=%wide.region_1.6_spmd.clone.sunk | while | flops 2154842624 | bytes 101166816 | solution.py:44
  220.7 11.0 %gather_fusion.2 = bf16[64,128,1024]{2,1,0:T(8,128)(2,1)} fusion(bf16[32,128,1024]{2,1,0:T(8,128)(2,1)} %get-tuple-element.137, s32[1024]{0:T(1024)S(1)} %pad_clamp_fusion.6), kind=kCustom, calls=%fused_computation.2.clone.clone.1 | custom fusion | bytes 33554688 | tf_op jit(solution)/shard_map/while/body/eval_jaxpr/gather | solution.py:34
  231.7 11.0 %gather_fusion.3 = bf16[64,128,1024]{2,1,0:T(8,128)(2,1)} fusion(bf16[32,128,1024]{2,1,0:T(8,128)(2,1)} %get-tuple-element.137, s32[1024]{0:T(1024)S(1)} %pad_clamp_fusion.5), kind=kCustom, calls=%fused_computation.3.clone.clone.1 | custom fusion | bytes 33554688 | tf_op jit(solution)/shard_map/while/body/eval_jaxpr/gather | solution.py:34
  242.6 13.1 %fusion.23 = (f32[64,128]{1,0:T(8,128)S(1)}, f32[64,128]{1,0:T(8,128)S(1)}) fusion(s32[64,128]{1,0:T(8,128)S(1)} %gather_fusion, s32[64,128]{1,0:T(8,128)S(1)} %gather_fusion.1, pred[128,128]{1,0:T(8,128)(4,1)S(1)} %iota_compare_fusion.2, pred[64]{0:T(512)(128)(4,1)S(1)} %compare_bitcast_fusion.2, bf16[64,128,1024]{2,1,0:T(8,128)(2,1)} %gather_fusion.2, ...), kind=kOutput, calls=%fused_computation.11.clone.1 | convolution fusion | flops 2154807296 | bytes 33701952 | tf_op jit(solution)/shard_map/while/body/eval_jaxpr/gid,gjd->gij/dot_general | solution.py:33
  255.7 2.2 scatter_fusion
  261.3 11.0 %gather_fusion.2 = bf16[64,128,1024]{2,1,0:T(8,128)(2,1)} fusion(bf16[32,128,1024]{2,1,0:T(8,128)(2,1)} %get-tuple-element.137, s32[1024]{0:T(1024)S(1)} %pad_clamp_fusion.6), kind=kCustom, calls=%fused_computation.2.clone.clone.1 | custom fusion | bytes 33554688 | tf_op jit(solution)/shard_map/while/body/eval_jaxpr/gather | solution.py:34
  272.3 10.9 %gather_fusion.3 = bf16[64,128,1024]{2,1,0:T(8,128)(2,1)} fusion(bf16[32,128,1024]{2,1,0:T(8,128)(2,1)} %get-tuple-element.137, s32[1024]{0:T(1024)S(1)} %pad_clamp_fusion.5), kind=kCustom, calls=%fused_computation.3.clone.clone.1 | custom fusion | bytes 33554688 | tf_op jit(solution)/shard_map/while/body/eval_jaxpr/gather | solution.py:34
  283.2 13.1 %fusion.23 = (f32[64,128]{1,0:T(8,128)S(1)}, f32[64,128]{1,0:T(8,128)S(1)}) fusion(s32[64,128]{1,0:T(8,128)S(1)} %gather_fusion, s32[64,128]{1,0:T(8,128)S(1)} %gather_fusion.1, pred[128,128]{1,0:T(8,128)(4,1)S(1)} %iota_compare_fusion.2, pred[64]{0:T(512)(128)(4,1)S(1)} %compare_bitcast_fusion.2, bf16[64,128,1024]{2,1,0:T(8,128)(2,1)} %gather_fusion.2, ...), kind=kOutput, calls=%fused_computation.11.clone.1 | convolution fusion | flops 2154807296 | bytes 33701952 | tf_op jit(solution)/shard_map/while/body/eval_jaxpr/gid,gjd->gij/dot_general | solution.py:33
  296.3 2.2 scatter_fusion
  301.9 10.9 %gather_fusion.2 = bf16[64,128,1024]{2,1,0:T(8,128)(2,1)} fusion(bf16[32,128,1024]{2,1,0:T(8,128)(2,1)} %get-tuple-element.137, s32[1024]{0:T(1024)S(1)} %pad_clamp_fusion.6), kind=kCustom, calls=%fused_computation.2.clone.clone.1 | custom fusion | bytes 33554688 | tf_op jit(solution)/shard_map/while/body/eval_jaxpr/gather | solution.py:34
  312.8 11.0 %gather_fusion.3 = bf16[64,128,1024]{2,1,0:T(8,128)(2,1)} fusion(bf16[32,128,1024]{2,1,0:T(8,128)(2,1)} %get-tuple-element.137, s32[1024]{0:T(1024)S(1)} %pad_clamp_fusion.5), kind=kCustom, calls=%fused_computation.3.clone.clone.1 | custom fusion | bytes 33554688 | tf_op jit(solution)/shard_map/while/body/eval_jaxpr/gather | solution.py:34
  323.7 13.1 %fusion.23 = (f32[64,128]{1,0:T(8,128)S(1)}, f32[64,128]{1,0:T(8,128)S(1)}) fusion(s32[64,128]{1,0:T(8,128)S(1)} %gather_fusion, s32[64,128]{1,0:T(8,128)S(1)} %gather_fusion.1, pred[128,128]{1,0:T(8,128)(4,1)S(1)} %iota_compare_fusion.2, pred[64]{0:T(512)(128)(4,1)S(1)} %compare_bitcast_fusion.2, bf16[64,128,1024]{2,1,0:T(8,128)(2,1)} %gather_fusion.2, ...), kind=kOutput, calls=%fused_computation.11.clone.1 | convolution fusion | flops 2154807296 | bytes 33701952 | tf_op jit(solution)/shard_map/while/body/eval_jaxpr/gid,gjd->gij/dot_general | solution.py:33
  336.8 2.2 scatter_fusion
  342.4 10.9 %gather_fusion.2 = bf16[64,128,1024]{2,1,0:T(8,128)(2,1)} fusion(bf16[32,128,1024]{2,1,0:T(8,128)(2,1)} %get-tuple-element.137, s32[1024]{0:T(1024)S(1)} %pad_clamp_fusion.6), kind=kCustom, calls=%fused_computation.2.clone.clone.1 | custom fusion | bytes 33554688 | tf_op jit(solution)/shard_map/while/body/eval_jaxpr/gather | solution.py:34
  353.3 11.0 %gather_fusion.3 = bf16[64,128,1024]{2,1,0:T(8,128)(2,1)} fusion(bf16[32,128,1024]{2,1,0:T(8,128)(2,1)} %get-tuple-element.137, s32[1024]{0:T(1024)S(1)} %pad_clamp_fusion.5), kind=kCustom, calls=%fused_computation.3.clone.clone.1 | custom fusion | bytes 33554688 | tf_op jit(solution)/shard_map/while/body/eval_jaxpr/gather | solution.py:34
  364.3 13.1 %fusion.23 = (f32[64,128]{1,0:T(8,128)S(1)}, f32[64,128]{1,0:T(8,128)S(1)}) fusion(s32[64,128]{1,0:T(8,128)S(1)} %gather_fusion, s32[64,128]{1,0:T(8,128)S(1)} %gather_fusion.1, pred[128,128]{1,0:T(8,128)(4,1)S(1)} %iota_compare_fusion.2, pred[64]{0:T(512)(128)(4,1)S(1)} %compare_bitcast_fusion.2, bf16[64,128,1024]{2,1,0:T(8,128)(2,1)} %gather_fusion.2, ...), kind=kOutput, calls=%fused_computation.11.clone.1 | convolution fusion | flops 2154807296 | bytes 33701952 | tf_op jit(solution)/shard_map/while/body/eval_jaxpr/gid,gjd->gij/dot_general | solution.py:33
  383.0 11.0 %gather_fusion.2 = bf16[64,128,1024]{2,1,0:T(8,128)(2,1)} fusion(bf16[32,128,1024]{2,1,0:T(8,128)(2,1)} %get-tuple-element.137, s32[1024]{0:T(1024)S(1)} %pad_clamp_fusion.6), kind=kCustom, calls=%fused_computation.2.clone.clone.1 | custom fusion | bytes 33554688 | tf_op jit(solution)/shard_map/while/body/eval_jaxpr/gather | solution.py:34
  393.9 11.0 %gather_fusion.3 = bf16[64,128,1024]{2,1,0:T(8,128)(2,1)} fusion(bf16[32,128,1024]{2,1,0:T(8,128)(2,1)} %get-tuple-element.137, s32[1024]{0:T(1024)S(1)} %pad_clamp_fusion.5), kind=kCustom, calls=%fused_computation.3.clone.clone.1 | custom fusion | bytes 33554688 | tf_op jit(solution)/shard_map/while/body/eval_jaxpr/gather | solution.py:34
  404.9 13.1 %fusion.23 = (f32[64,128]{1,0:T(8,128)S(1)}, f32[64,128]{1,0:T(8,128)S(1)}) fusion(s32[64,128]{1,0:T(8,128)S(1)} %gather_fusion, s32[64,128]{1,0:T(8,128)S(1)} %gather_fusion.1, pred[128,128]{1,0:T(8,128)(4,1)S(1)} %iota_compare_fusion.2, pred[64]{0:T(512)(128)(4,1)S(1)} %compare_bitcast_fusion.2, bf16[64,128,1024]{2,1,0:T(8,128)(2,1)} %gather_fusion.2, ...), kind=kOutput, calls=%fused_computation.11.clone.1 | convolution fusion | flops 2154807296 | bytes 33701952 | tf_op jit(solution)/shard_map/while/body/eval_jaxpr/gid,gjd->gij/dot_general | solution.py:33
  418.0 2.2 scatter_fusion
  423.6 11.0 %gather_fusion.2 = bf16[64,128,1024]{2,1,0:T(8,128)(2,1)} fusion(bf16[32,128,1024]{2,1,0:T(8,128)(2,1)} %get-tuple-element.137, s32[1024]{0:T(1024)S(1)} %pad_clamp_fusion.6), kind=kCustom, calls=%fused_computation.2.clone.clone.1 | custom fusion | bytes 33554688 | tf_op jit(solution)/shard_map/while/body/eval_jaxpr/gather | solution.py:34
  434.6 10.9 %gather_fusion.3 = bf16[64,128,1024]{2,1,0:T(8,128)(2,1)} fusion(bf16[32,128,1024]{2,1,0:T(8,128)(2,1)} %get-tuple-element.137, s32[1024]{0:T(1024)S(1)} %pad_clamp_fusion.5), kind=kCustom, calls=%fused_computation.3.clone.clone.1 | custom fusion | bytes 33554688 | tf_op jit(solution)/shard_map/while/body/eval_jaxpr/gather | solution.py:34
  445.5 13.1 %fusion.23 = (f32[64,128]{1,0:T(8,128)S(1)}, f32[64,128]{1,0:T(8,128)S(1)}) fusion(s32[64,128]{1,0:T(8,128)S(1)} %gather_fusion, s32[64,128]{1,0:T(8,128)S(1)} %gather_fusion.1, pred[128,128]{1,0:T(8,128)(4,1)S(1)} %iota_compare_fusion.2, pred[64]{0:T(512)(128)(4,1)S(1)} %compare_bitcast_fusion.2, bf16[64,128,1024]{2,1,0:T(8,128)(2,1)} %gather_fusion.2, ...), kind=kOutput, calls=%fused_computation.11.clone.1 | convolution fusion | flops 2154807296 | bytes 33701952 | tf_op jit(solution)/shard_map/while/body/eval_jaxpr/gid,gjd->gij/dot_general | solution.py:33
  458.6 2.2 scatter_fusion
  462.9 2.5 all-to-all-start.3
  466.1 6.5 %all-to-all-done.3 = f32[32,1,128]{2,1,0:T(1,128)S(1)} async-done(((f32[32,1,128]{2,1,0:T(1,128)}), f32[32,1,128]{2,1,0:T(1,128)S(1)}, u32[]{:S(2)}, u32[]{:S(2)}) %all-to-all-start.3) | async-done | bytes 16416 | tf_op jit(solution)/shard_map/all_to_all | solution.py:47
  (78 shorter events, 32.6 us)
Async XLA Ops:
  0.0 17.0 %copy-start = (s32[256]{0:T(256)S(1)}, s32[256]{0:T(256)}, u32[]{:S(2)}) copy-start(s32[256]{0:T(256)} %param.8) | copy-start | bytes 3076
  1.3 14.4 %all-to-all-start = ((s32[32,1,1]{2,1,0:T(1,128)}), s32[32,1,1]{2,1,0:T(1,128)S(1)}, u32[]{:S(2)}, u32[]{:S(2)}) async-start(s32[32,1,1]{2,1,0:T(1,128)} %copy.8), calls=%async_computation | async-start | bytes 32768 | tf_op jit(solution)/shard_map/all_to_all | solution.py:20
  15.8 2.4 copy-start.1
  16.5 0.6 copy-start.5
  18.2 9.6 %all-to-all-start.1 = ((bf16[32,1,128]{2,1,0:T(2,128)(2,1)}), bf16[32,1,128]{2,1,0:T(2,128)(2,1)S(1)}, u32[]{:S(2)}, u32[]{:S(2)}) async-start(bf16[32,1,128]{2,1,0:T(2,128)(2,1)} %copy.9), calls=%async_computation.1 | async-start | bytes 32768 | tf_op jit(solution)/shard_map/all_to_all | solution.py:26
  21.9 10.9 %copy-start.3 = (s32[384]{0:T(512)S(1)}, s32[384]{0:T(512)}, u32[]{:S(2)}) copy-start(s32[384]{0:T(512)} %param.10) | copy-start | bytes 4612
  21.9 10.9 %copy-start.4 = (s32[384]{0:T(512)S(1)}, s32[384]{0:T(512)}, u32[]{:S(2)}) copy-start(s32[384]{0:T(512)} %param.11) | copy-start | bytes 4612
  27.8 191.0 %all-to-all-start.2 = ((bf16[32,128,1024]{2,1,0:T(8,128)(2,1)}), bf16[32,128,1024]{2,1,0:T(8,128)(2,1)}, u32[]{:S(2)}, u32[]{:S(2)}) async-start(bf16[32,128,1024]{2,1,0:T(8,128)(2,1)} %gather_fusion.5), calls=%async_computation.2 | async-start | bytes 16777216 | tf_op jit(solution)/shard_map/all_to_all | solution.py:25
  219.4 246.0 %copy-start.2 = (s32[32,1,1]{2,1,0:T(1,128)S(1)}, s32[32,1,1]{2,1,0:T(1,128)}, u32[]{:S(2)}) copy-start(s32[32,1,1]{2,1,0:T(1,128)} %copy-done.1) | copy-start | bytes 388
  462.9 9.7 %all-to-all-start.3 = ((f32[32,1,128]{2,1,0:T(1,128)}), f32[32,1,128]{2,1,0:T(1,128)S(1)}, u32[]{:S(2)}, u32[]{:S(2)}) async-start(f32[32,1,128]{2,1,0:T(1,128)} %bitcast.6), calls=%async_computation.3 | async-start | bytes 32768 | tf_op jit(solution)/shard_map/all_to_all | solution.py:47
where the time goes:
time: 475 us; the launch traced here: 474 us
  waiting for transfers between devices  199 us (42%)
  local copies, waits for them, and re-layouts  147 us (31%)
  matrix products  78.5 us (17%)
  other arithmetic  31.4 us (7%)
  starting transfers between devices  17.2 us (4%)
    all_to_all x1, waiting for transfers between devices, local(): lax.all_to_all(outgoing, 'dev', split_axis=0, concat_axis=0, tiled=True)  186 us
    dot_general x6, matrix products, step(): jnp.einsum('gid,gjd->gij', fetched[left], fetched[right], preferred_eleme...  78.5 us
    gather x6, local copies, waits for them, and re-layouts, step(): fetched[left]  65.8 us
    gather x6, local copies, waits for them, and re-layouts, step(): fetched[right]  65.7 us
    another operation x6, other arithmetic, step(): carry = carry.at[left].max(jnp.max(sims, axis=2))  12.9 us
    another operation x6, other arithmetic, step(): carry = carry.at[right].max(jnp.max(sims, axis=1))  12.9 us
  transfers between devices with their start and end apart: 4, of which 4 were waited for; matrix products, arithmetic and copies ran while one was open for 2% of the time, Pallas kernels for 0%

commit v1 on v0

v1 whole, which is shorter than its diff:
```python
import functools

import jax
import jax.numpy as jnp
from jax import lax
from jax.experimental import pallas as pl
from jax.experimental.pallas import tpu as pltpu
from jax.sharding import PartitionSpec as P

BLOCK = 128
CLUSTERS = 16
PLANE = 8
AXIS = "dev"


def normalise_kernel(x_ref, unit_ref):
    values = x_ref[...].astype(jnp.float32)
    norm = lax.rsqrt(jnp.sum(values * values, axis=-1, keepdims=True) + 1e-06)
    unit_ref[...] = (values * norm).astype(jnp.bfloat16)


def normalise(x):
    return pl.pallas_call(
        normalise_kernel,
        out_shape=jax.ShapeDtypeStruct(x.shape, jnp.bfloat16),
        compiler_params=pltpu.CompilerParams(vmem_limit_bytes=16 * 1024 * 1024),
    )(x)


def tile_kernel(n_right, n_left, own_first, info_ref, *refs):
    rights, lefts, outs = refs[:n_right], refs[n_right : n_right + n_left], refs[n_right + n_left :]
    rows = rights[0].shape[0]

    def label_of(index):
        label = jnp.zeros(index.shape, jnp.int32)
        for c in range(1, CLUSTERS):
            label += (index >= info_ref[c]).astype(jnp.int32)
        return label

    lane = lax.broadcasted_iota(jnp.int32, (1, rows), 1)
    right_labels = [label_of(lane + info_ref[CLUSTERS + r]) for r in range(n_right)]
    for out in outs:
        out[...] = jnp.full(out.shape, -1.0, jnp.float32)
    for c in range(n_left):
        base = info_ref[CLUSTERS + n_right + c]
        index = lax.broadcasted_iota(jnp.int32, (rows, BLOCK), 0) + base
        label = jnp.where(base < 0, -1, label_of(index))
        label = jnp.concatenate([label] * (rows // BLOCK), axis=1)
        for r in range(n_right):
            sims = lax.dot_general(
                lefts[c][...], rights[r][...], (((1,), (1,)), ((), ())), preferred_element_type=jnp.float32
            )
            same = label == right_labels[r]
            if own_first and c == 0 and r == 0:
                same &= lax.broadcasted_iota(jnp.int32, sims.shape, 0) != lax.broadcasted_iota(
                    jnp.int32, sims.shape, 1
                )
            sims = jnp.where(same, sims, -1.0)
            for b in range(rows // BLOCK):
                at = c * (rows // BLOCK) + b
                outs[r][at : at + 1, :] = jnp.max(
                    sims[b * BLOCK : (b + 1) * BLOCK], axis=0, keepdims=True
                )


def tiles(rights, lefts, starts, right_bases, left_bases, own_first):
    rows, depth = rights[0].shape
    height = -(-len(lefts) * (rows // BLOCK) // 8) * 8
    info = jnp.concatenate([starts, jnp.stack(list(right_bases) + list(left_bases))]).astype(jnp.int32)
    n = len(rights) + len(lefts)
    return pl.pallas_call(
        functools.partial(tile_kernel, len(rights), len(lefts), own_first),
        in_specs=[pl.BlockSpec(memory_space=pltpu.SMEM)] + [pl.BlockSpec(memory_space=pltpu.VMEM)] * n,
        out_specs=[pl.BlockSpec(memory_space=pltpu.VMEM)] * len(rights),
        out_shape=[jax.ShapeDtypeStruct((height, rows), jnp.float32)] * len(rights),
        compiler_params=pltpu.CompilerParams(vmem_limit_bytes=32 * 1024 * 1024),
        cost_estimate=pl.CostEstimate(
            flops=2 * len(rights) * len(lefts) * rows * rows * depth,
            bytes_accessed=2 * n * rows * depth,
            transcendentals=0,
        ),
    )(info, *rights, *lefts)


def local(embeddings, cluster_id, requests, pair_left, pair_right):
    n = lax.axis_size(AXIS)
    me = lax.axis_index(AXIS)
    rows = embeddings.shape[0]
    blk_dev = rows // BLOCK
    n_planes = n // PLANE
    place, plane = me % PLANE, me // PLANE

    def swap(x, bit):
        return lax.ppermute(x, AXIS, [(i, i ^ bit) for i in range(n)])

    def from_above(x):
        return lax.ppermute(x, AXIS, [(i + PLANE, i) for i in range(n - PLANE)])

    def from_below(x):
        return lax.ppermute(x, AXIS, [(i, i + PLANE) for i in range(n - PLANE)])

    unit = normalise(embeddings)
    along_x, along_y = swap(unit, 2), swap(unit, 4)
    above, below = from_above(unit), from_below(unit)
    twin = swap(unit, 1)
    half = rows // 2
    across = jnp.concatenate([swap(along_x[:half], 4), swap(along_y[half:], 2)], axis=0)
    above_twin, below_twin = swap(above, 1), swap(below, 1)

    slots = jnp.arange(n, dtype=jnp.int32)
    left_hot = (slots[:, None] == pair_left[None, :]).astype(jnp.bfloat16)
    right_hot = (slots[:, None] == pair_right[None, :]).astype(jnp.bfloat16)
    listed = jnp.einsum("sp,tp->st", left_hot, right_hot, preferred_element_type=jnp.float32)
    listed = listed + listed.T
    counts = jnp.sum(
        (cluster_id[None, :] == jnp.arange(CLUSTERS, dtype=jnp.int32)[:, None]).astype(jnp.float32), axis=1
    )
    tail = jnp.concatenate([requests.astype(jnp.float32), counts])
    message = jnp.concatenate([listed, jnp.broadcast_to(tail[None], (n, tail.shape[0]))], axis=1)
    width = message.shape[1]
    message = jnp.pad(message, ((0, 0), (0, -width % BLOCK)))[:, None, :]
    heard = lax.all_to_all(message, AXIS, split_axis=0, concat_axis=0, tiled=True)[:, 0, :]
    heard_listed = heard[:, :n] > 0
    heard_requests = heard[:, n : 2 * n].astype(jnp.int32)
    counts = jnp.sum(heard[:, 2 * n : 2 * n + CLUSTERS], axis=0).astype(jnp.int32)
    ends = jnp.cumsum(counts)
    starts = ends - counts
    per_plane = rows * PLANE
    span = jnp.max(jnp.where(counts > 0, (ends - 1) // per_plane - starts // per_plane, 0))
    own_request = jnp.sum(jnp.where(slots[None, :] == me, heard_requests, 0), axis=1)
    blocks = jnp.arange(blk_dev, dtype=jnp.int32)
    covered = jnp.any(
        heard_listed[:, :, None, None]
        & (heard_requests[:, :, None, None] == blocks[None, None, :, None])
        & (own_request[:, None, None, None] == blocks[None, None, None, :]),
        axis=0,
    )
    covered = covered.reshape(n_planes, PLANE, blk_dev, blk_dev)
    covered = jnp.take(covered, jnp.arange(PLANE) ^ place, axis=1)
    caps = jnp.where(covered, jnp.float32(jnp.inf), jnp.float32(-1.0))
    caps = jnp.repeat(caps, BLOCK, axis=-1)
    caps = jnp.pad(caps, ((n_planes, n_planes), (0, 0), (0, 0), (0, 0)), constant_values=-1.0)

    def caps_of(offset):
        cap = lax.dynamic_index_in_dim(caps, plane + n_planes + offset, 0, keepdims=False)
        return cap.reshape(PLANE // 2, 2 * blk_dev, rows)

    def base_of(device, offset):
        at = plane + offset
        inside = (at >= 0) & (at < n_planes)
        return jnp.where(inside, (device + offset * PLANE) * rows, -1)

    right_bases = [(me ^ bit) * rows for bit in (0, 2, 4, 6)]

    lefts = [unit, twin, above, above_twin, below, below_twin]
    left_bases = [base_of(me ^ bit, offset) for offset in (0, 1, -1) for bit in (0, 1)]
    mine, for_x, for_y = tiles([unit, along_x, along_y], lefts, starts, right_bases[:3], left_bases, True)
    (for_across,) = tiles([across], lefts, starts, right_bases[3:], left_bases, False)
    near = jnp.stack([mine, swap(for_x, 2), swap(for_y, 4), swap(for_across, 6)])
    cap = jnp.concatenate([caps_of(0), caps_of(1), caps_of(-1)], axis=1)
    best = jnp.max(jnp.minimum(near[:, : cap.shape[1]], cap), axis=(0, 1))

    def further(best):
        def body(carry):
            offset, best, above, below = carry
            above, below = from_above(above), from_below(below)
            lefts = [above, swap(above, 1), below, swap(below, 1)]
            left_bases = [base_of(me ^ bit, o) for o in (offset, -offset) for bit in (0, 1)]
            mine, for_x, for_y, for_across = tiles(
                [unit, along_x, along_y, across], lefts, starts, right_bases, left_bases, False
            )
            far = jnp.stack([mine, swap(for_x, 2), swap(for_y, 4), swap(for_across, 6)])
            cap = jnp.concatenate([caps_of(offset), caps_of(-offset)], axis=1)
            best = jnp.maximum(best, jnp.max(jnp.minimum(far[:, : cap.shape[1]], cap), axis=(0, 1)))
            return offset + 1, best, above, below

        return lax.while_loop(lambda carry: carry[0] <= span, body, (jnp.int32(2), best, above, below))[1]

    best = lax.cond(span >= 2, further, lambda best: best, best)
    return jnp.maximum(best, -1.0)


def solution(mesh):
    in_specs = (P(AXIS, None), P(AXIS), P(AXIS), P(AXIS), P(AXIS))
    return jax.shard_map(local, mesh=mesh, in_specs=in_specs, out_specs=P(AXIS), check_vma=False)
```

time: 475 us -> 54.3 us (0.11)
  waiting for transfers between devices: 199 us -> 15.6 us
  local copies, waits for them, and re-layouts: 147 us -> 6.12 us
  matrix products: 78.5 us -> 0.13 us
  other arithmetic: 31.4 us -> 2.18 us
  Pallas kernels: 0 us -> 8.41 us
    all_to_all x4 -> x1, waiting for transfers between devices: 199 us -> 7 us  [local(): lax.all_to_all(message, AXIS, split_axis=0, concat_axis=0, tiled=True)]
    gather x26 -> x1, local copies, waits for them, and re-layouts: 144 us -> 0.58 us  [local(): covered = jnp.take(covered, jnp.arange(PLANE) ^ place, axis=1)]
    dot_general x6 -> x1, matrix products: 78.5 us -> 0.13 us  [local(): jnp.einsum('sp,tp->st', left_hot, right_hot, preferred_element_type=jnp.f...]
    another operation x13 -> x2, other arithmetic: 27.3 us -> 0.16 us  [the longest x6 12.9 us: step(): carry = carry.at[left].max(jnp.max(sims, axis=2))]
    ppermute x0 -> x12, starting transfers between devices: none -> 17.6 us  [the longest x10 11 us: swap(): return lax.ppermute(x, AXIS, [(i, i ^ bit) for i in range(n)])]
    all_to_all x4 -> x1, starting transfers between devices: 17.2 us -> 2.99 us  [local(): lax.all_to_all(message, AXIS, split_axis=0, concat_axis=0, tiled=True)]
    ppermute x0 -> x12, waiting for transfers between devices: none -> 8.56 us  [the longest x10 8.55 us: swap(): return lax.ppermute(x, AXIS, [(i, i ^ bit) for i in range(n)])]
    pallas_call x0 -> x3, Pallas kernels: none -> 8.41 us  [the longest x2 8.22 us: tiles(): pl.pallas_call(functools.partial(tile_kernel, len(rights), len(lefts), ow...]
  transfers between devices with their start and end apart: 4 -> 13, of which waited for: 4 -> 5; matrix products, arithmetic and copies ran while one was open for 2% -> 10% of each run, Pallas kernels for 0% -> 9%
where the time goes in v1:
time: 54.3 us; the launch traced here: 54 us
  starting transfers between devices  20.6 us (38%)
  waiting for transfers between devices  15.6 us (29%)
  Pallas kernels  8.41 us (15%)
  local copies, waits for them, and re-layouts  6.12 us (11%)
  other arithmetic  2.18 us (4%)
  between operations  1 us (2%)
    ppermute x10, starting transfers between devices, swap(): return lax.ppermute(x, AXIS, [(i, i ^ bit) for i in range(n)])  11 us
    ppermute x10, waiting for transfers between devices, swap(): return lax.ppermute(x, AXIS, [(i, i ^ bit) for i in range(n)])  8.55 us
    pallas_call x2, Pallas kernels, tiles(): pl.pallas_call(functools.partial(tile_kernel, len(rights), len(lefts), ow...  8.22 us
    all_to_all x1, waiting for transfers between devices, local(): lax.all_to_all(message, AXIS, split_axis=0, concat_axis=0, tiled=True)  7 us
    ppermute x1, starting transfers between devices, from_below(): return lax.ppermute(x, AXIS, [(i, i + PLANE) for i in range(n - PLANE)])  5.34 us
    all_to_all x1, starting transfers between devices, local(): lax.all_to_all(message, AXIS, split_axis=0, concat_axis=0, tiled=True)  2.99 us
    unnamed x15, local copies, waits for them, and re-layouts  2.29 us
    slice x1, local copies, waits for them, and re-layouts, local(): along_y[half:]  1.67 us
  transfers between devices with their start and end apart: 13, of which 5 were waited for; matrix products, arithmetic and copies ran while one was open for 10% of the time, Pallas kernels for 9%

profile of v1, /device:TPU:0, one launch (start us, length us, event | category | flops | bytes accessed | tf_op | source)
XLA Modules:
  0.0 54.0 jit_solution(9055423481165538923)
XLA Ops:
  0.0 1.0 %copy-done = bf16[256,1024]{1,0:T(8,128)(2,1)S(1)} copy-done((bf16[256,1024]{1,0:T(8,128)(2,1)S(1)}, bf16[256,1024]{1,0:T(8,128)(2,1)}, u32[]{:S(2)}) %copy-start) | copy-done | bytes 524312
  1.0 0.2 shard_map.55.refs_0_.refs_3_.refs_1_
  1.2 3.0 %collective-permute-start.7 = (bf16[256,1024]{1,0:T(8,128)(2,1)S(1)}, bf16[256,1024]{1,0:T(8,128)(2,1)S(1)}, u32[]{:S(2)}, u32[]{:S(2)}) collective-permute-start(bf16[256,1024]{1,0:T(8,128)(2,1)S(1)} %shard_map.55.refs_0_.refs_3_.refs_1_), channel_id=1, source_target_pairs={{0,2},{1,3},{2,0},{3,1},{4,6},{5,7},{6,4},{7,5},{8,10},{9,11},{10,... | collective-permute-start | bytes 1572872 | tf_op jit(solution)/shard_map/ppermute | solution.py:94
  4.2 1.5 %collective-permute-start.8 = (bf16[256,1024]{1,0:T(8,128)(2,1)S(1)}, bf16[256,1024]{1,0:T(8,128)(2,1)}, u32[]{:S(2)}, u32[]{:S(2)}) collective-permute-start(bf16[256,1024]{1,0:T(8,128)(2,1)S(1)} %shard_map.55.refs_0_.refs_3_.refs_1_), channel_id=1, source_target_pairs={{0,4},{1,5},{2,6},{3,7},{4,0},{5,1},{6,2},{7,3},{8,12},{9,13},{10,... | collective-permute-start | bytes 1572872 | tf_op jit(solution)/shard_map/ppermute | solution.py:94
  5.8 1.3 %collective-permute-start.10 = (bf16[256,1024]{1,0:T(8,128)(2,1)S(1)}, bf16[256,1024]{1,0:T(8,128)(2,1)}, u32[]{:S(2)}, u32[]{:S(2)}) collective-permute-start(bf16[256,1024]{1,0:T(8,128)(2,1)S(1)} %shard_map.55.refs_0_.refs_3_.refs_1_), channel_id=1, source_target_pairs={{8,0},{9,1},{10,2},{11,3},{12,4},{13,5},{14,6},{15,7},{16,8},{17,9... | collective-permute-start | bytes 1572872 | tf_op jit(solution)/shard_map/ppermute | solution.py:97
  7.1 5.3 %collective-permute-start.12 = (bf16[256,1024]{1,0:T(8,128)(2,1)S(1)}, bf16[256,1024]{1,0:T(8,128)(2,1)}, u32[]{:S(2)}, u32[]{:S(2)}) collective-permute-start(bf16[256,1024]{1,0:T(8,128)(2,1)S(1)} %shard_map.55.refs_0_.refs_3_.refs_1_), channel_id=1, source_target_pairs={{0,8},{1,9},{2,10},{3,11},{4,12},{5,13},{6,14},{7,15},{8,16},{9,17... | collective-permute-start | bytes 1572872 | tf_op jit(solution)/shard_map/ppermute | solution.py:100
  12.4 0.1 fusion.3
  12.6 0.7 %copy-done.5 = s32[256]{0:T(256)S(1)} copy-done((s32[256]{0:T(256)S(1)}, s32[256]{0:T(256)}, u32[]{:S(2)}) %copy-start.5) | copy-done | bytes 1048
  13.4 0.5 copy-done.6
  14.0 0.6 %pad.8 = f32[32,128]{1,0:T(8,128)} pad(f32[32,80]{1,0:T(8,128)S(1)} %pad_maximum_fusion.3, f32[]{:T(128)} %constant.125.clone.1), padding=0_0x0_48 | pad | bytes 26628 | tf_op jit(solution)/shard_map/jit(_pad)/pad | solution.py:121
  14.7 3.0 %all-to-all-start = ((f32[32,1,128]{2,1,0:T(1,128)}), f32[32,1,128]{2,1,0:T(1,128)S(1)}, u32[]{:S(2)}, u32[]{:S(2)}) async-start(f32[32,1,128]{2,1,0:T(1,128)} %bitcast.13), calls=%async_computation | async-start | bytes 32768 | tf_op jit(solution)/shard_map/all_to_all | solution.py:122
  17.8 7.0 %all-to-all-done = f32[32,1,128]{2,1,0:T(1,128)S(1)} async-done(((f32[32,1,128]{2,1,0:T(1,128)}), f32[32,1,128]{2,1,0:T(1,128)S(1)}, u32[]{:S(2)}, u32[]{:S(2)}) %all-to-all-start) | async-done | bytes 16416 | tf_op jit(solution)/shard_map/all_to_all | solution.py:122
  24.9 0.2 select_reduce_fusion
  25.3 0.1 copy.19
  25.4 0.6 %gather_fusion = pred[8,4,2,2]{3,1,2,0:T(4,128)(4,1)S(1)} fusion(pred[4,8,2,2]{3,0,2,1:T(4,128)(4,1)S(1)} %copy.19, s32[1024]{0:T(1024)S(1)} %pad_clamp_fusion), kind=kCustom, calls=%fused_computation | custom fusion | bytes 288 | tf_op jit(solution)/shard_map/jit(_take)/gather | solution.py:139
  26.2 0.9 %collective-permute-start.16 = (bf16[128,1024]{1,0:T(8,128)(2,1)S(1)}, bf16[128,1024]{1,0:T(8,128)(2,1)S(1)}, u32[]{:S(2)}, u32[]{:S(2)}) collective-permute-start(bf16[128,1024]{1,0:T(8,128)(2,1)S(1)} %slice.27), channel_id=1, source_target_pairs={{0,4},{1,5},{2,6},{3,7},{4,0},{5,1},{6,2},{7,3},{8,12},{9,13},{10,... | collective-permute-start | bytes 786440 | tf_op jit(solution)/shard_map/ppermute | solution.py:94
  27.2 0.5 collective-permute-start.13
  27.8 0.1 reduce
  27.9 0.1 broadcast_in_dim.64
  28.2 1.7 %slice.28 = bf16[128,1024]{1,0:T(8,128)(2,1)} slice(bf16[256,1024]{1,0:T(8,128)(2,1)} %collective-permute-done.8.refs_2_), slice={[128:256], [0:1024]} | slice | bytes 524288 | tf_op jit(solution)/shard_map/slice | solution.py:107
  29.8 1.4 %collective-permute-start.17 = (bf16[128,1024]{1,0:T(8,128)(2,1)}, bf16[128,1024]{1,0:T(8,128)(2,1)S(1)}, u32[]{:S(2)}, u32[]{:S(2)}) collective-permute-start(bf16[128,1024]{1,0:T(8,128)(2,1)} %slice.28), channel_id=1, source_target_pairs={{0,2},{1,3},{2,0},{3,1},{4,6},{5,7},{6,4},{7,5},{8,10},{9,11},{10,... | collective-permute-start | bytes 786440 | tf_op jit(solution)/shard_map/ppermute | solution.py:94
  31.3 0.6 %convert_subtract_fusion = (s32[16]{0:T(128)S(1)}, s32[]{:T(128)}) fusion(s32[16]{0:T(128)S(1)} %reduce, f32[16]{0:T(128)S(1)} %slice_reduce_fusion), kind=kLoop, calls=%fused_computation.51 | loop fusion | flops 591 | bytes 196 | tf_op jit(solution)/shard_map/sub | solution.py:127
  32.1 2.3 %collective-permute-done.16 = bf16[128,1024]{1,0:T(8,128)(2,1)S(1)} collective-permute-done((bf16[128,1024]{1,0:T(8,128)(2,1)S(1)}, bf16[128,1024]{1,0:T(8,128)(2,1)S(1)}, u32[]{:S(2)}, u32[]{:S(2)}) %collective-permute-start.16) | collective-permute-done | bytes 262176 | tf_op jit(solution)/shard_map/ppermute | solution.py:94
  34.4 3.9 %collective-permute-done.17 = bf16[128,1024]{1,0:T(8,128)(2,1)S(1)} collective-permute-done((bf16[128,1024]{1,0:T(8,128)(2,1)}, bf16[128,1024]{1,0:T(8,128)(2,1)S(1)}, u32[]{:S(2)}, u32[]{:S(2)}) %collective-permute-start.17) | collective-permute-done | bytes 262176 | tf_op jit(solution)/shard_map/ppermute | solution.py:94
  38.4 3.3 %shard_map.57 = f32[16,256]{1,0:T(8,128)S(1)} custom-call(s32[23]{0:T(128)S(1)} %concatenate.28.info_ref, bf16[256,1024]{1,0:T(8,128)(2,1)S(1)} %constant_dynamic-update-slice_fusion.refs_0_, bf16[256,1024]{1,0:T(8,128)(2,1)S(1)} %shard_map.55.refs_0_.refs_3_.refs_1_, bf16[256,1024]{1,0:T(8,128)(2,1)S(1)} %collective-permute-done.9.refs_4_.refs_2_, ...), custom_call_target="tpu_custom_call" | custom-call | flops 805306368 | bytes 3670016 | tf_op jit(solution)/shard_map/pallas_call | solution.py:71
  41.7 1.6 %collective-permute-start.18 = (f32[16,256]{1,0:T(8,128)S(1)}, f32[16,256]{1,0:T(8,128)S(1)}, u32[]{:S(2)}, u32[]{:S(2)}) collective-permute-start(f32[16,256]{1,0:T(8,128)S(1)} %shard_map.57), channel_id=1, source_target_pairs={{0,6},{1,7},{2,4},{3,5},{4,2},{5,3},{6,0},{7,1},{8,14},{9,15},{10,... | collective-permute-start | bytes 49160 | tf_op jit(solution)/shard_map/ppermute | solution.py:94
  43.3 4.9 %shard_map.56 = (f32[16,256]{1,0:T(8,128)S(1)}, f32[16,256]{1,0:T(8,128)S(1)}, f32[16,256]{1,0:T(8,128)S(1)}) custom-call(s32[25]{0:T(128)S(1)} %concatenate.27.info_ref, bf16[256,1024]{1,0:T(8,128)(2,1)S(1)} %shard_map.55.refs_0_.refs_3_.refs_1_, bf16[256,1024]{1,0:T(8,128)(2,1)S(1)} %copy-done.2, bf16[256,1024]{1,0:T(8,128)(2,1)} %collective-permute-done.8.refs_2_, ...), custom_call_target="tpu_custom_call" | custom-call | flops 2415919104 | bytes 4718592 | tf_op jit(solution)/shard_map/pallas_call | solution.py:71
  48.2 1.4 %collective-permute-start.15 = (f32[16,256]{1,0:T(8,128)S(1)}, f32[16,256]{1,0:T(8,128)S(1)}, u32[]{:S(2)}, u32[]{:S(2)}) collective-permute-start(f32[16,256]{1,0:T(8,128)S(1)} %get-tuple-element.228), channel_id=1, source_target_pairs={{0,4},{1,5},{2,6},{3,7},{4,0},{5,1},{6,2},{7,3},{8,12},{9,13},{10,... | collective-permute-start | bytes 49160 | tf_op jit(solution)/shard_map/ppermute | solution.py:94
  49.6 0.6 %collective-permute-start.14 = (f32[16,256]{1,0:T(8,128)S(1)}, f32[16,256]{1,0:T(8,128)S(1)}, u32[]{:S(2)}, u32[]{:S(2)}) collective-permute-start(f32[16,256]{1,0:T(8,128)S(1)} %get-tuple-element.227), channel_id=1, source_target_pairs={{0,2},{1,3},{2,0},{3,1},{4,6},{5,7},{6,4},{7,5},{8,10},{9,11},{10,... | collective-permute-start | bytes 49160 | tf_op jit(solution)/shard_map/ppermute | solution.py:94
  51.1 0.9 %collective-permute-done.15 = f32[16,256]{1,0:T(8,128)S(1)} collective-permute-done((f32[16,256]{1,0:T(8,128)S(1)}, f32[16,256]{1,0:T(8,128)S(1)}, u32[]{:S(2)}, u32[]{:S(2)}) %collective-permute-start.15) | collective-permute-done | bytes 16416 | tf_op jit(solution)/shard_map/ppermute | solution.py:94
  52.0 1.4 %collective-permute-done.14 = f32[16,256]{1,0:T(8,128)S(1)} collective-permute-done((f32[16,256]{1,0:T(8,128)S(1)}, f32[16,256]{1,0:T(8,128)S(1)}, u32[]{:S(2)}, u32[]{:S(2)}) %collective-permute-start.14) | collective-permute-done | bytes 16416 | tf_op jit(solution)/shard_map/ppermute | solution.py:94
  53.4 0.6 %broadcast_maximum_fusion = f32[256]{0:T(256)} fusion(f32[256]{0:T(256)S(1)} %get-tuple-element.480), kind=kLoop, calls=%fused_computation.49 | loop fusion | flops 256 | bytes 2048 | tf_op jit(solution)/shard_map/max | solution.py:180
  (56 shorter events, 1.4 us)
Async XLA Ops:
  0.0 1.0 %copy-start = (bf16[256,1024]{1,0:T(8,128)(2,1)S(1)}, bf16[256,1024]{1,0:T(8,128)(2,1)}, u32[]{:S(2)}) copy-start(bf16[256,1024]{1,0:T(8,128)(2,1)} %x_ref.1) | copy-start | bytes 1572868
  1.0 11.4 %copy-start.3 = (s32[384]{0:T(512)S(1)}, s32[384]{0:T(512)}, u32[]{:S(2)}) copy-start(s32[384]{0:T(512)} %param.13) | copy-start | bytes 4612
  1.0 11.4 %copy-start.4 = (s32[384]{0:T(512)S(1)}, s32[384]{0:T(512)}, u32[]{:S(2)}) copy-start(s32[384]{0:T(512)} %param.12) | copy-start | bytes 4612
  1.2 25.0 %collective-permute-start.7 = (bf16[256,1024]{1,0:T(8,128)(2,1)S(1)}, bf16[256,1024]{1,0:T(8,128)(2,1)S(1)}, u32[]{:S(2)}, u32[]{:S(2)}) collective-permute-start(bf16[256,1024]{1,0:T(8,128)(2,1)S(1)} %shard_map.55.refs_0_.refs_3_.refs_1_), channel_id=1, source_target_pairs={{0,2},{1,3},{2,0},{3,1},{4,6},{5,7},{6,4},{7,5},{8,10},{9,11},{10,... | collective-permute-start | bytes 1572872 | tf_op jit(solution)/shard_map/ppermute | solution.py:94
  4.2 23.9 %collective-permute-start.8 = (bf16[256,1024]{1,0:T(8,128)(2,1)S(1)}, bf16[256,1024]{1,0:T(8,128)(2,1)}, u32[]{:S(2)}, u32[]{:S(2)}) collective-permute-start(bf16[256,1024]{1,0:T(8,128)(2,1)S(1)} %shard_map.55.refs_0_.refs_3_.refs_1_), channel_id=1, source_target_pairs={{0,4},{1,5},{2,6},{3,7},{4,0},{5,1},{6,2},{7,3},{8,12},{9,13},{10,... | collective-permute-start | bytes 1572872 | tf_op jit(solution)/shard_map/ppermute | solution.py:94
  5.8 32.6 %collective-permute-start.9 = (bf16[256,1024]{1,0:T(8,128)(2,1)S(1)}, bf16[256,1024]{1,0:T(8,128)(2,1)S(1)}, u32[]{:S(2)}, u32[]{:S(2)}) collective-permute-start(bf16[256,1024]{1,0:T(8,128)(2,1)S(1)} %shard_map.55.refs_0_.refs_3_.refs_1_), channel_id=1, source_target_pairs={{0,1},{1,0},{2,3},{3,2},{4,5},{5,4},{6,7},{7,6},{8,9},{9,8},{10,11... | collective-permute-start | bytes 1572872 | tf_op jit(solution)/shard_map/ppermute | solution.py:94
  5.8 21.4 %collective-permute-start.10 = (bf16[256,1024]{1,0:T(8,128)(2,1)S(1)}, bf16[256,1024]{1,0:T(8,128)(2,1)}, u32[]{:S(2)}, u32[]{:S(2)}) collective-permute-start(bf16[256,1024]{1,0:T(8,128)(2,1)S(1)} %shard_map.55.refs_0_.refs_3_.refs_1_), channel_id=1, source_target_pairs={{8,0},{9,1},{10,2},{11,3},{12,4},{13,5},{14,6},{15,7},{16,8},{17,9... | collective-permute-start | bytes 1572872 | tf_op jit(solution)/shard_map/ppermute | solution.py:97
  7.1 20.1 %collective-permute-start.12 = (bf16[256,1024]{1,0:T(8,128)(2,1)S(1)}, bf16[256,1024]{1,0:T(8,128)(2,1)}, u32[]{:S(2)}, u32[]{:S(2)}) collective-permute-start(bf16[256,1024]{1,0:T(8,128)(2,1)S(1)} %shard_map.55.refs_0_.refs_3_.refs_1_), channel_id=1, source_target_pairs={{0,8},{1,9},{2,10},{3,11},{4,12},{5,13},{6,14},{7,15},{8,16},{9,17... | collective-permute-start | bytes 1572872 | tf_op jit(solution)/shard_map/ppermute | solution.py:100
  12.6 0.7 %copy-start.5 = (s32[256]{0:T(256)S(1)}, s32[256]{0:T(256)}, u32[]{:S(2)}) copy-start(s32[256]{0:T(256)} %param.10) | copy-start | bytes 3076
  13.3 0.7 %copy-start.6 = (s32[32]{0:T(128)S(1)}, s32[32]{0:T(128)}, u32[]{:S(2)}) copy-start(s32[32]{0:T(128)} %param.11) | copy-start | bytes 388
  14.7 10.1 %all-to-all-start = ((f32[32,1,128]{2,1,0:T(1,128)}), f32[32,1,128]{2,1,0:T(1,128)S(1)}, u32[]{:S(2)}, u32[]{:S(2)}) async-start(f32[32,1,128]{2,1,0:T(1,128)} %bitcast.13), calls=%async_computation | async-start | bytes 32768 | tf_op jit(solution)/shard_map/all_to_all | solution.py:122
  26.2 0.9 %copy-start.1 = (bf16[256,1024]{1,0:T(8,128)(2,1)}, bf16[256,1024]{1,0:T(8,128)(2,1)S(1)}, u32[]{:S(2)}) copy-start(bf16[256,1024]{1,0:T(8,128)(2,1)S(1)} %collective-permute-done.7.refs_1_) | copy-start | bytes 1572868
  26.2 8.1 %collective-permute-start.16 = (bf16[128,1024]{1,0:T(8,128)(2,1)S(1)}, bf16[128,1024]{1,0:T(8,128)(2,1)S(1)}, u32[]{:S(2)}, u32[]{:S(2)}) collective-permute-start(bf16[128,1024]{1,0:T(8,128)(2,1)S(1)} %slice.27), channel_id=1, source_target_pairs={{0,4},{1,5},{2,6},{3,7},{4,0},{5,1},{6,2},{7,3},{8,12},{9,13},{10,... | collective-permute-start | bytes 786440 | tf_op jit(solution)/shard_map/ppermute | solution.py:94
  27.2 11.2 %collective-permute-start.11 = (bf16[256,1024]{1,0:T(8,128)(2,1)}, bf16[256,1024]{1,0:T(8,128)(2,1)S(1)}, u32[]{:S(2)}, u32[]{:S(2)}) collective-permute-start(bf16[256,1024]{1,0:T(8,128)(2,1)} %collective-permute-done.10.refs_5_.refs_3_), channel_id=1, source_target_pairs={{0,1},{1,0},{2,3},{3,2},{4,5},{5,4},{6,7},{7,6},{8,9},{9,8},{10,11... | collective-permute-start | bytes 1572872 | tf_op jit(solution)/shard_map/ppermute | solution.py:94
  27.2 11.2 %collective-permute-start.13 = (bf16[256,1024]{1,0:T(8,128)(2,1)}, bf16[256,1024]{1,0:T(8,128)(2,1)S(1)}, u32[]{:S(2)}, u32[]{:S(2)}) collective-permute-start(bf16[256,1024]{1,0:T(8,128)(2,1)} %collective-permute-done.12.refs_7_.refs_5_), channel_id=1, source_target_pairs={{0,1},{1,0},{2,3},{3,2},{4,5},{5,4},{6,7},{7,6},{8,9},{9,8},{10,11... | collective-permute-start | bytes 1572872 | tf_op jit(solution)/shard_map/ppermute | solution.py:94
  29.8 8.5 %collective-permute-start.17 = (bf16[128,1024]{1,0:T(8,128)(2,1)}, bf16[128,1024]{1,0:T(8,128)(2,1)S(1)}, u32[]{:S(2)}, u32[]{:S(2)}) collective-permute-start(bf16[128,1024]{1,0:T(8,128)(2,1)} %slice.28), channel_id=1, source_target_pairs={{0,2},{1,3},{2,0},{3,1},{4,6},{5,7},{6,4},{7,5},{8,10},{9,11},{10,... | collective-permute-start | bytes 786440 | tf_op jit(solution)/shard_map/ppermute | solution.py:94
  38.4 5.0 %copy-start.2 = (bf16[256,1024]{1,0:T(8,128)(2,1)S(1)}, bf16[256,1024]{1,0:T(8,128)(2,1)}, u32[]{:S(2)}) copy-start(bf16[256,1024]{1,0:T(8,128)(2,1)} %copy-done.1) | copy-start | bytes 1572868
  41.7 9.3 %collective-permute-start.18 = (f32[16,256]{1,0:T(8,128)S(1)}, f32[16,256]{1,0:T(8,128)S(1)}, u32[]{:S(2)}, u32[]{:S(2)}) collective-permute-start(f32[16,256]{1,0:T(8,128)S(1)} %shard_map.57), channel_id=1, source_target_pairs={{0,6},{1,7},{2,4},{3,5},{4,2},{5,3},{6,0},{7,1},{8,14},{9,15},{10,... | collective-permute-start | bytes 49160 | tf_op jit(solution)/shard_map/ppermute | solution.py:94
  48.2 3.8 %collective-permute-start.15 = (f32[16,256]{1,0:T(8,128)S(1)}, f32[16,256]{1,0:T(8,128)S(1)}, u32[]{:S(2)}, u32[]{:S(2)}) collective-permute-start(f32[16,256]{1,0:T(8,128)S(1)} %get-tuple-element.228), channel_id=1, source_target_pairs={{0,4},{1,5},{2,6},{3,7},{4,0},{5,1},{6,2},{7,3},{8,12},{9,13},{10,... | collective-permute-start | bytes 49160 | tf_op jit(solution)/shard_map/ppermute | solution.py:94
  49.6 3.7 %collective-permute-start.14 = (f32[16,256]{1,0:T(8,128)S(1)}, f32[16,256]{1,0:T(8,128)S(1)}, u32[]{:S(2)}, u32[]{:S(2)}) collective-permute-start(f32[16,256]{1,0:T(8,128)S(1)} %get-tuple-element.227), channel_id=1, source_target_pairs={{0,2},{1,3},{2,0},{3,1},{4,6},{5,7},{6,4},{7,5},{8,10},{9,11},{10,... | collective-permute-start | bytes 49160 | tf_op jit(solution)/shard_map/ppermute | solution.py:94

commit v2 on v1

v2 whole, which is shorter than its diff:
```python
import functools

import jax
import jax.numpy as jnp
from jax import lax
from jax.experimental import pallas as pl
from jax.experimental.pallas import tpu as pltpu
from jax.sharding import PartitionSpec as P

BLOCK = 128
CLUSTERS = 16
PLANE = 8
LAST_COST = 10_000_000_000
JOIN_COST = 10_000_000_000
AXIS = "dev"
LABEL_ROWS = 16
VMEM_TILES = 8 * 1024 * 1024


def normalise_kernel(x_hbm, cluster_hbm, unit_ref, x_ref, cluster_ref, sems):
    copies = [
        pltpu.make_async_copy(x_hbm, x_ref, sems.at[0]),
        pltpu.make_async_copy(cluster_hbm, cluster_ref, sems.at[1]),
    ]
    for copy in copies:
        copy.start()
    rows, depth = x_ref.shape
    unit_ref[rows:] = jnp.zeros((LABEL_ROWS, depth), jnp.bfloat16)
    copies[1].wait()
    label = (cluster_ref[...] + 1).astype(jnp.bfloat16)
    unit_ref[rows:, :rows] = jnp.broadcast_to(label, (LABEL_ROWS, rows))
    copies[0].wait()
    values = x_ref[...].astype(jnp.float32)
    norm = lax.rsqrt(jnp.sum(values * values, axis=-1, keepdims=True) + 1e-06)
    unit_ref[:rows] = (values * norm).astype(jnp.bfloat16)


def normalise(x, cluster_id):
    rows, depth = x.shape
    return pl.pallas_call(
        normalise_kernel,
        in_specs=[pl.BlockSpec(memory_space=pltpu.HBM)] * 2,
        out_shape=jax.ShapeDtypeStruct((rows + LABEL_ROWS, depth), jnp.bfloat16),
        scratch_shapes=[
            pltpu.VMEM((rows, depth), x.dtype),
            pltpu.VMEM((1, rows), jnp.int32),
            pltpu.SemaphoreType.DMA((2,)),
        ],
        compiler_params=pltpu.CompilerParams(vmem_limit_bytes=60 * 1024 * 1024),
    )(x, cluster_id.reshape(1, rows))


def message_kernel(n, left_ref, right_ref, request_ref, cluster_ref, out_ref):
    def dot(a, b):
        return lax.dot_general(a, b, (((1,), (1,)), ((), ())), preferred_element_type=jnp.float32)

    def hot(count, ref):
        index = lax.broadcasted_iota(jnp.int32, (count, ref.shape[1]), 0)
        return (index == ref[...]).astype(jnp.float32).astype(jnp.bfloat16)

    left, right, cluster = hot(n, left_ref), hot(n, right_ref), hot(CLUSTERS, cluster_ref)
    out_ref[...] = jnp.zeros(out_ref.shape, jnp.float32)
    out_ref[:, 0, :n] = dot(left, right) + dot(right, left)
    out_ref[:, 0, n : 2 * n] = jnp.broadcast_to(request_ref[...].astype(jnp.float32), (n, n))
    counts = dot(jnp.ones((n, cluster.shape[1]), jnp.bfloat16), cluster)
    out_ref[:, 0, 2 * n : 2 * n + CLUSTERS] = counts


def message_of(requests, pair_left, pair_right, cluster_id):
    n = requests.shape[0]
    width = -(-(2 * n + CLUSTERS) // BLOCK) * BLOCK
    return pl.pallas_call(
        functools.partial(message_kernel, n),
        out_shape=jax.ShapeDtypeStruct((n, 1, width), jnp.float32),
        compiler_params=pltpu.CompilerParams(vmem_limit_bytes=4 * 1024 * 1024),
    )(pair_left.reshape(1, -1), pair_right.reshape(1, -1), requests.reshape(1, -1), cluster_id.reshape(1, -1))


def halves_kernel(x_ref, y_ref, first_ref, second_ref):
    first_ref[...] = x_ref[: first_ref.shape[0]]
    second_ref[...] = y_ref[first_ref.shape[0] :]


def halves(x, y):
    half = (x.shape[0] - LABEL_ROWS) // 2
    return pl.pallas_call(
        halves_kernel,
        out_shape=[
            jax.ShapeDtypeStruct((half, x.shape[1]), x.dtype),
            jax.ShapeDtypeStruct((half + LABEL_ROWS, x.shape[1]), x.dtype),
        ],
        compiler_params=pltpu.CompilerParams(vmem_limit_bytes=4 * 1024 * 1024),
        cost_estimate=pl.CostEstimate(flops=0, bytes_accessed=x.size * 4, transcendentals=0),
    )(x, y)


def join_kernel(first_ref, second_ref, x_ref):
    x_ref[: first_ref.shape[0]] = first_ref[...]
    x_ref[first_ref.shape[0] :] = second_ref[...]


def join(first, second):
    return pl.pallas_call(
        join_kernel,
        out_shape=jax.ShapeDtypeStruct((first.shape[0] + second.shape[0], first.shape[1]), first.dtype),
        compiler_params=pltpu.CompilerParams(vmem_limit_bytes=4 * 1024 * 1024),
        cost_estimate=pl.CostEstimate(flops=JOIN_COST, bytes_accessed=first.size * 8, transcendentals=0),
    )(first, second)


def tile_kernel(n_right, places, rows, own_first, n_before, *refs):
    right_refs, refs = refs[:n_right], refs[n_right:]
    left_refs, refs = refs[: len(places)], refs[len(places) :]
    before, outs = refs[: n_before], refs[n_before :]
    right_rows = [right[:rows] for right in right_refs]
    right_labels = [right[rows:, :rows].astype(jnp.float32)[:1] for right in right_refs]
    for r, out in enumerate(outs):
        out[...] = jnp.full(out.shape, -1.0, jnp.float32)
        if r < n_before:
            out[: before[r].shape[0]] = before[r][...]
    blocks = rows // BLOCK
    for c, left in enumerate(left_refs):
        left_label = left[rows:, :rows].astype(jnp.float32)[:1]
        for r, out in enumerate(outs):
            if r < n_before and places[c] < before[r].shape[0]:
                continue
            sims = lax.dot_general(
                left[:rows], right_rows[r], (((1,), (1,)), ((), ())), preferred_element_type=jnp.float32
            )
            for b in range(blocks):
                at = slice(b * BLOCK, (b + 1) * BLOCK)
                label = jnp.broadcast_to(left_label[:, at], (BLOCK, BLOCK)).T
                label = jnp.concatenate([label] * blocks, axis=1)
                same = label == right_labels[r]
                part = sims[at]
                if own_first and c == 0 and r == 0:
                    index = lax.broadcasted_iota(jnp.int32, part.shape, 0) + b * BLOCK
                    same &= index != lax.broadcasted_iota(jnp.int32, part.shape, 1)
                part = jnp.where(same, part, -1.0)
                row = places[c] + b
                out[row : row + 1, :] = jnp.max(part, axis=0, keepdims=True)


def tiles(rights, lefts, places, own_first, before=(), flops=None):
    rows, depth = lefts[0].shape
    rows -= LABEL_ROWS
    height = -(-(places[-1] + rows // BLOCK) // 8) * 8
    if flops is None:
        flops = 2 * len(rights) * len(lefts) * rows * rows * depth
    operands = list(rights) + list(lefts) + list(before)
    return pl.pallas_call(
        functools.partial(tile_kernel, len(rights), tuple(places), rows, own_first, len(before)),
        in_specs=[pl.BlockSpec(memory_space=pltpu.VMEM)] * len(operands),
        out_specs=[pl.BlockSpec(memory_space=pltpu.VMEM)] * len(rights),
        out_shape=[jax.ShapeDtypeStruct((height, rows), jnp.float32)] * len(rights),
        compiler_params=pltpu.CompilerParams(vmem_limit_bytes=VMEM_TILES),
        cost_estimate=pl.CostEstimate(
            flops=flops, bytes_accessed=2 * len(operands) * rows * depth, transcendentals=0
        ),
    )(*operands)


def local(embeddings, cluster_id, requests, pair_left, pair_right):
    n = lax.axis_size(AXIS)
    me = lax.axis_index(AXIS)
    rows = embeddings.shape[0]
    blk_dev = rows // BLOCK
    n_planes = n // PLANE
    place, plane = me % PLANE, me // PLANE

    def swap(x, bit):
        return lax.ppermute(x, AXIS, [(i, i ^ bit) for i in range(n)])

    def from_above(x):
        return lax.ppermute(x, AXIS, [(i + PLANE, i) for i in range(n - PLANE)])

    def from_below(x):
        return lax.ppermute(x, AXIS, [(i, i + PLANE) for i in range(n - PLANE)])

    unit = normalise(embeddings, cluster_id)
    along_x, along_y = swap(unit, 2), swap(unit, 4)
    above, below = from_above(unit), from_below(unit)
    twin = swap(unit, 1)
    first, second = halves(along_x, along_y)
    pieces = [swap(first, 4), swap(second, 2)]
    along_x, first = lax.optimization_barrier((along_x, first))
    near_rights = [unit, along_x, along_y]
    plane_places = [0, blk_dev]
    next_places = [8 + blk_dev * k for k in range(4)]
    plane_parts = list(tiles(near_rights, [unit, twin], plane_places, True))
    above_twin, below_twin = swap(above, 1), swap(below, 1)

    slots = jnp.arange(n, dtype=jnp.int32)
    message = message_of(requests, pair_left, pair_right, cluster_id)
    heard = lax.all_to_all(message, AXIS, split_axis=0, concat_axis=0, tiled=True)[:, 0, :]
    lefts = [above, above_twin, below, below_twin]
    mine, for_x, for_y = tiles(near_rights, lefts, next_places, False, plane_parts)
    across = join(*pieces)
    (for_across,) = tiles([across], [unit, twin] + lefts, plane_places + next_places, False, flops=LAST_COST)
    heard, mine = lax.optimization_barrier((heard, mine))
    near = jnp.stack([mine, swap(for_x, 2), swap(for_y, 4), swap(for_across, 6)])
    heard_listed = heard[:, :n] > 0
    heard_requests = heard[:, n : 2 * n].astype(jnp.int32)
    counts = jnp.sum(heard[:, 2 * n : 2 * n + CLUSTERS], axis=0).astype(jnp.int32)
    ends = jnp.cumsum(counts)
    starts = ends - counts
    per_plane = rows * PLANE
    span = jnp.max(jnp.where(counts > 0, (ends - 1) // per_plane - starts // per_plane, 0))
    own_request = jnp.sum(jnp.where(slots[None, :] == me, heard_requests, 0), axis=1)
    blocks = jnp.arange(blk_dev, dtype=jnp.int32)
    covered = jnp.any(
        heard_listed[:, :, None, None]
        & (heard_requests[:, :, None, None] == blocks[None, None, :, None])
        & (own_request[:, None, None, None] == blocks[None, None, None, :]),
        axis=0,
    )
    covered = covered.reshape(n_planes, PLANE, blk_dev, blk_dev)
    covered = jnp.take(covered, jnp.arange(PLANE) ^ place, axis=1)
    caps = jnp.where(covered, jnp.float32(jnp.inf), jnp.float32(-1.0))
    caps = jnp.repeat(caps, BLOCK, axis=-1)
    caps = jnp.pad(caps, ((n_planes, n_planes), (0, 0), (0, 0), (0, 0)), constant_values=-1.0)

    def caps_of(offset):
        cap = lax.dynamic_index_in_dim(caps, plane + n_planes + offset, 0, keepdims=False)
        return cap.reshape(PLANE // 2, 2 * blk_dev, rows)

    cap = jnp.pad(caps_of(0), ((0, 0), (0, 8 - 2 * blk_dev), (0, 0)), constant_values=-1.0)
    cap = jnp.concatenate([cap, caps_of(1), caps_of(-1)], axis=1)
    best = jnp.max(jnp.minimum(near, cap), axis=(0, 1))

    def further(best):
        def body(carry):
            offset, best, above, below = carry
            above, below = from_above(above), from_below(below)
            lefts = [above, swap(above, 1), below, swap(below, 1)]
            mine, for_x, for_y, for_across = tiles(
                near_rights + [across], lefts, [blk_dev * k for k in range(4)], False
            )
            far = jnp.stack([mine, swap(for_x, 2), swap(for_y, 4), swap(for_across, 6)])
            cap = jnp.concatenate([caps_of(offset), caps_of(-offset)], axis=1)
            best = jnp.maximum(best, jnp.max(jnp.minimum(far[:, : cap.shape[1]], cap), axis=(0, 1)))
            return offset + 1, best, above, below

        return lax.while_loop(lambda carry: carry[0] <= span, body, (jnp.int32(2), best, above, below))[1]

    best = lax.cond(span >= 2, further, lambda best: best, best)
    return jnp.maximum(best, -1.0)


def solution(mesh):
    in_specs = (P(AXIS, None), P(AXIS), P(AXIS), P(AXIS), P(AXIS))
    return jax.shard_map(local, mesh=mesh, in_specs=in_specs, out_specs=P(AXIS), check_vma=False)
```

time: 54.3 us -> 44.4 us (0.82)
  waiting for transfers between devices: 15.6 us -> 8.16 us
  local copies, waits for them, and re-layouts: 6.12 us -> 1.97 us
  Pallas kernels: 8.41 us -> 11.5 us
  starting transfers between devices: 20.6 us -> 19.5 us
    all_to_all x1, waiting for transfers between devices: 7 us -> 0.01 us  [local(): lax.all_to_all(message, AXIS, split_axis=0, concat_axis=0, tiled=True)]
    pallas_call x3 -> x7, Pallas kernels: 8.41 us -> 11.5 us  [the longest x3 7.44 us: tiles(): pl.pallas_call(functools.partial(tile_kernel, len(rights), tuple(places),...]
    slice x2 -> x0, local copies, waits for them, and re-layouts: 1.69 us -> none  [the longest x1 1.67 us: local(): along_y[half:]]
    unnamed x15 -> x14, local copies, waits for them, and re-layouts: 2.29 us -> 0.69 us
    ppermute x10, waiting for transfers between devices: 8.55 us -> 7.16 us  [swap(): return lax.ppermute(x, AXIS, [(i, i ^ bit) for i in range(n)])]
    ppermute x1, waiting for transfers between devices: 0.01 us -> 1 us  [from_below(): return lax.ppermute(x, AXIS, [(i, i + PLANE) for i in range(n - PLANE)])]
    ppermute x10, starting transfers between devices: 11 us -> 10.3 us  [swap(): return lax.ppermute(x, AXIS, [(i, i ^ bit) for i in range(n)])]
    sub x1 -> x0, other arithmetic: 0.64 us -> none  [local(): starts = ends - counts]
  transfers between devices with their start and end apart: 13 -> 13, of which waited for: 5 -> 7; matrix products, arithmetic and copies ran while one was open for 10% -> 2% of each run, Pallas kernels for 9% -> 18%
where the time goes in v2:
time: 44.4 us; the launch traced here: 44.1 us
  starting transfers between devices  19.5 us (44%)
  Pallas kernels  11.5 us (26%)
  waiting for transfers between devices  8.16 us (18%)
  local copies, waits for them, and re-layouts  1.97 us (4%)
  other arithmetic  1.97 us (4%)
  between operations  0.95 us (2%)
    ppermute x10, starting transfers between devices, swap(): return lax.ppermute(x, AXIS, [(i, i ^ bit) for i in range(n)])  10.3 us
    pallas_call x3, Pallas kernels, tiles(): pl.pallas_call(functools.partial(tile_kernel, len(rights), tuple(places),...  7.44 us
    ppermute x10, waiting for transfers between devices, swap(): return lax.ppermute(x, AXIS, [(i, i ^ bit) for i in range(n)])  7.16 us
    ppermute x1, starting transfers between devices, from_below(): return lax.ppermute(x, AXIS, [(i, i + PLANE) for i in range(n - PLANE)])  5.38 us
    all_to_all x1, starting transfers between devices, local(): lax.all_to_all(message, AXIS, split_axis=0, concat_axis=0, tiled=True)  2.54 us
    ppermute x1, starting transfers between devices, from_above(): return lax.ppermute(x, AXIS, [(i + PLANE, i) for i in range(n - PLANE)])  1.28 us
    pallas_call x1, Pallas kernels, normalise(): pl.pallas_call(normalise_kernel, in_specs=[pl.BlockSpec(memory_space=pltp...  1.26 us
    pallas_call x1, Pallas kernels, halves(): pl.pallas_call(halves_kernel, out_shape=[jax.ShapeDtypeStruct((half, x.sh...  1.09 us
  transfers between devices with their start and end apart: 13, of which 7 were waited for; matrix products, arithmetic and copies ran while one was open for 2% of the time, Pallas kernels for 18%

profile of v2, /device:TPU:0, one launch (start us, length us, event | category | flops | bytes accessed | tf_op | source)
XLA Modules:
  0.0 44.1 jit_solution(3828765980379876349)
XLA Ops:
  0.0 1.3 %shard_map.56.refs_0_.refs_3_.refs_1_ = bf16[272,1024]{1,0:T(8,128)(2,1)S(1)} custom-call(bf16[256,1024]{1,0:T(8,128)(2,1)} %x_hbm.1, s32[1,256]{1,0:T(1,128)} %bitcast.29), custom_call_target="tpu_custom_call" | custom-call | tf_op jit(solution)/shard_map/pallas_call | solution.py:40
  1.3 3.0 %collective-permute-start.7 = (bf16[272,1024]{1,0:T(8,128)(2,1)S(1)}, bf16[272,1024]{1,0:T(8,128)(2,1)S(1)}, u32[]{:S(2)}, u32[]{:S(2)}) collective-permute-start(bf16[272,1024]{1,0:T(8,128)(2,1)S(1)} %shard_map.56.refs_0_.refs_3_.refs_1_), channel_id=1, source_target_pairs={{0,2},{1,3},{2,0},{3,1},{4,6},{5,7},{6,4},{7,5},{8,10},{9,11},{10,... | collective-permute-start | bytes 1671176 | tf_op jit(solution)/shard_map/ppermute | solution.py:172
  4.3 1.5 %collective-permute-start.8 = (bf16[272,1024]{1,0:T(8,128)(2,1)S(1)}, bf16[272,1024]{1,0:T(8,128)(2,1)}, u32[]{:S(2)}, u32[]{:S(2)}) collective-permute-start(bf16[272,1024]{1,0:T(8,128)(2,1)S(1)} %shard_map.56.refs_0_.refs_3_.refs_1_), channel_id=1, source_target_pairs={{0,4},{1,5},{2,6},{3,7},{4,0},{5,1},{6,2},{7,3},{8,12},{9,13},{10,... | collective-permute-start | bytes 1671176 | tf_op jit(solution)/shard_map/ppermute | solution.py:172
  5.8 1.3 %collective-permute-start.9 = (bf16[272,1024]{1,0:T(8,128)(2,1)S(1)}, bf16[272,1024]{1,0:T(8,128)(2,1)S(1)}, u32[]{:S(2)}, u32[]{:S(2)}) collective-permute-start(bf16[272,1024]{1,0:T(8,128)(2,1)S(1)} %shard_map.56.refs_0_.refs_3_.refs_1_), channel_id=1, source_target_pairs={{8,0},{9,1},{10,2},{11,3},{12,4},{13,5},{14,6},{15,7},{16,8},{17,9... | collective-permute-start | bytes 1671176 | tf_op jit(solution)/shard_map/ppermute | solution.py:175
  7.1 5.4 %collective-permute-start.11 = (bf16[272,1024]{1,0:T(8,128)(2,1)S(1)}, bf16[272,1024]{1,0:T(8,128)(2,1)}, u32[]{:S(2)}, u32[]{:S(2)}) collective-permute-start(bf16[272,1024]{1,0:T(8,128)(2,1)S(1)} %shard_map.56.refs_0_.refs_3_.refs_1_), channel_id=1, source_target_pairs={{0,8},{1,9},{2,10},{3,11},{4,12},{5,13},{6,14},{7,15},{8,16},{9,17... | collective-permute-start | bytes 1671176 | tf_op jit(solution)/shard_map/ppermute | solution.py:178
  12.5 0.7 %copy-done = s32[256]{0:T(256)S(1)} copy-done((s32[256]{0:T(256)S(1)}, s32[256]{0:T(256)}, u32[]{:S(2)}) %copy-start) | copy-done | bytes 1048
  13.2 0.8 %shard_map.55 = f32[32,1,128]{2,1,0:T(1,128)} custom-call(s32[1,384]{1,0:T(1,128)S(1)} %reshape.131.left_ref, s32[1,384]{1,0:T(1,128)S(1)} %reshape.132.right_ref, s32[1,32]{1,0:T(1,128)S(1)} %bitcast.31, s32[1,256]{1,0:T(1,128)S(1)} %bitcast.30), custom_call_target="tpu_custom_call" | custom-call | tf_op jit(solution)/shard_map/pallas_call | solution.py:72
  14.0 2.5 %all-to-all-start = ((f32[32,1,128]{2,1,0:T(1,128)}), f32[32,1,128]{2,1,0:T(1,128)S(1)}, u32[]{:S(2)}, u32[]{:S(2)}) async-start(f32[32,1,128]{2,1,0:T(1,128)} %shard_map.55), calls=%async_computation | async-start | bytes 32768 | tf_op jit(solution)/shard_map/all_to_all | solution.py:195
  16.7 0.3 collective-permute-done.7.x_ref.refs_1_
  16.9 1.6 %collective-permute-done.8.y_ref.refs_2_ = bf16[272,1024]{1,0:T(8,128)(2,1)} collective-permute-done((bf16[272,1024]{1,0:T(8,128)(2,1)S(1)}, bf16[272,1024]{1,0:T(8,128)(2,1)}, u32[]{:S(2)}, u32[]{:S(2)}) %collective-permute-start.8) | collective-permute-done | bytes 557088 | tf_op jit(solution)/shard_map/ppermute | solution.py:172
  18.5 1.1 %shard_map.57 = (bf16[128,1024]{1,0:T(8,128)(2,1)S(1)}, bf16[144,1024]{1,0:T(8,128)(2,1)S(1)}) custom-call(bf16[272,1024]{1,0:T(8,128)(2,1)S(1)} %collective-permute-done.7.x_ref.refs_1_, bf16[272,1024]{1,0:T(8,128)(2,1)} %collective-permute-done.8.y_ref.refs_2_), custom_call_target="tpu_custom_call" | custom-call | bytes 1114112 | tf_op jit(solution)/shard_map/pallas_call | solution.py:86
  19.6 1.6 %collective-permute-start.16 = (bf16[128,1024]{1,0:T(8,128)(2,1)S(1)}, bf16[128,1024]{1,0:T(8,128)(2,1)S(1)}, u32[]{:S(2)}, u32[]{:S(2)}) collective-permute-start(bf16[128,1024]{1,0:T(8,128)(2,1)S(1)} %get-tuple-element.180), channel_id=1, source_target_pairs={{0,4},{1,5},{2,6},{3,7},{4,0},{5,1},{6,2},{7,3},{8,12},{9,13},{10,... | collective-permute-start | bytes 786440 | tf_op jit(solution)/shard_map/ppermute | solution.py:172
  21.2 0.5 %collective-permute-start.17 = (bf16[144,1024]{1,0:T(8,128)(2,1)S(1)}, bf16[144,1024]{1,0:T(8,128)(2,1)S(1)}, u32[]{:S(2)}, u32[]{:S(2)}) collective-permute-start(bf16[144,1024]{1,0:T(8,128)(2,1)S(1)} %get-tuple-element.190), channel_id=1, source_target_pairs={{0,2},{1,3},{2,0},{3,1},{4,6},{5,7},{6,4},{7,5},{8,10},{9,11},{10,... | collective-permute-start | bytes 884744 | tf_op jit(solution)/shard_map/ppermute | solution.py:172
  21.8 1.0 %collective-permute-done.11.refs_5_ = bf16[272,1024]{1,0:T(8,128)(2,1)} collective-permute-done((bf16[272,1024]{1,0:T(8,128)(2,1)S(1)}, bf16[272,1024]{1,0:T(8,128)(2,1)}, u32[]{:S(2)}, u32[]{:S(2)}) %collective-permute-start.11) | collective-permute-done | bytes 557088 | tf_op jit(solution)/shard_map/ppermute | solution.py:178
  22.8 2.1 %shard_map.58 = (f32[8,256]{1,0:T(8,128)S(1)}, f32[8,256]{1,0:T(8,128)S(1)}, f32[8,256]{1,0:T(8,128)S(1)}) custom-call(bf16[272,1024]{1,0:T(8,128)(2,1)S(1)} %shard_map.56.refs_0_.refs_3_.refs_1_, bf16[272,1024]{1,0:T(8,128)(2,1)S(1)} %collective-permute-done.7.x_ref.refs_1_, bf16[272,1024]{1,0:T(8,128)(2,1)} %collective-permute-done.8.y_ref.refs_2_, ...), custom_call_target="tpu_custom_call" | custom-call | flops 805306368 | bytes 2621440 | tf_op jit(solution)/shard_map/pallas_call | solution.py:151
  24.9 1.7 %collective-permute-done.16.first_ref = bf16[128,1024]{1,0:T(8,128)(2,1)S(1)} collective-permute-done((bf16[128,1024]{1,0:T(8,128)(2,1)S(1)}, bf16[128,1024]{1,0:T(8,128)(2,1)S(1)}, u32[]{:S(2)}, u32[]{:S(2)}) %collective-permute-start.16) | collective-permute-done | bytes 262176 | tf_op jit(solution)/shard_map/ppermute | solution.py:172
  26.6 1.9 %collective-permute-done.17.second_ref = bf16[144,1024]{1,0:T(8,128)(2,1)S(1)} collective-permute-done((bf16[144,1024]{1,0:T(8,128)(2,1)S(1)}, bf16[144,1024]{1,0:T(8,128)(2,1)S(1)}, u32[]{:S(2)}, u32[]{:S(2)}) %collective-permute-start.17) | collective-permute-done | bytes 294944 | tf_op jit(solution)/shard_map/ppermute | solution.py:172
  28.5 0.9 %shard_map.60.refs_0_ = bf16[272,1024]{1,0:T(8,128)(2,1)} custom-call(bf16[128,1024]{1,0:T(8,128)(2,1)S(1)} %collective-permute-done.16.first_ref, bf16[144,1024]{1,0:T(8,128)(2,1)S(1)} %collective-permute-done.17.second_ref), custom_call_target="tpu_custom_call" | custom-call | flops 10000000000 | bytes 1048576 | tf_op jit(solution)/shard_map/pallas_call | solution.py:103
  29.4 3.1 %shard_map.59 = (f32[16,256]{1,0:T(8,128)S(1)}, f32[16,256]{1,0:T(8,128)S(1)}, f32[16,256]{1,0:T(8,128)S(1)}) custom-call(bf16[272,1024]{1,0:T(8,128)(2,1)S(1)} %shard_map.56.refs_0_.refs_3_.refs_1_, bf16[272,1024]{1,0:T(8,128)(2,1)S(1)} %collective-permute-done.7.x_ref.refs_1_, bf16[272,1024]{1,0:T(8,128)(2,1)} %collective-permute-done.8.y_ref.refs_2_, ...), custom_call_target="tpu_custom_call" | custom-call | flops 1610612736 | bytes 5242880 | tf_op jit(solution)/shard_map/pallas_call | solution.py:151
  32.8 0.1 reduce
  33.0 0.2 select_reduce_fusion
  33.4 0.1 copy.12
  33.5 0.6 %gather_fusion = pred[8,4,2,2]{3,1,2,0:T(4,128)(4,1)S(1)} fusion(pred[4,8,2,2]{3,0,2,1:T(4,128)(4,1)S(1)} %copy.12, s32[1024]{0:T(1024)S(1)} %pad_clamp_fusion), kind=kCustom, calls=%fused_computation | custom fusion | bytes 288 | tf_op jit(solution)/shard_map/jit(_take)/gather | solution.py:218
  34.2 0.1 broadcast_in_dim.47
  34.4 2.3 %shard_map.61 = f32[16,256]{1,0:T(8,128)S(1)} custom-call(bf16[272,1024]{1,0:T(8,128)(2,1)} %shard_map.60.refs_0_, bf16[272,1024]{1,0:T(8,128)(2,1)S(1)} %shard_map.56.refs_0_.refs_3_.refs_1_, bf16[272,1024]{1,0:T(8,128)(2,1)S(1)} %collective-permute-done.13.refs_4_.refs_2_, bf16[272,1024]{1,0:T(8,128)(2,1)S(1)} %collective-permute-done.9.refs_3_, ...), custom_call_target="tpu_custom_call" | custom-call | flops 10000000000 | bytes 3670016 | tf_op jit(solution)/shard_map/pallas_call | solution.py:151
  36.7 1.5 %collective-permute-start.18 = (f32[16,256]{1,0:T(8,128)S(1)}, f32[16,256]{1,0:T(8,128)S(1)}, u32[]{:S(2)}, u32[]{:S(2)}) collective-permute-start(f32[16,256]{1,0:T(8,128)S(1)} %shard_map.61), channel_id=1, source_target_pairs={{0,6},{1,7},{2,4},{3,5},{4,2},{5,3},{6,0},{7,1},{8,14},{9,15},{10,... | collective-permute-start | bytes 49160 | tf_op jit(solution)/shard_map/ppermute | solution.py:172
  38.2 1.5 %collective-permute-start.15 = (f32[16,256]{1,0:T(8,128)S(1)}, f32[16,256]{1,0:T(8,128)S(1)}, u32[]{:S(2)}, u32[]{:S(2)}) collective-permute-start(f32[16,256]{1,0:T(8,128)S(1)} %get-tuple-element.189), channel_id=1, source_target_pairs={{0,4},{1,5},{2,6},{3,7},{4,0},{5,1},{6,2},{7,3},{8,12},{9,13},{10,... | collective-permute-start | bytes 49160 | tf_op jit(solution)/shard_map/ppermute | solution.py:172
  39.7 0.6 %collective-permute-start.14 = (f32[16,256]{1,0:T(8,128)S(1)}, f32[16,256]{1,0:T(8,128)S(1)}, u32[]{:S(2)}, u32[]{:S(2)}) collective-permute-start(f32[16,256]{1,0:T(8,128)S(1)} %get-tuple-element.188), channel_id=1, source_target_pairs={{0,2},{1,3},{2,0},{3,1},{4,6},{5,7},{6,4},{7,5},{8,10},{9,11},{10,... | collective-permute-start | bytes 49160 | tf_op jit(solution)/shard_map/ppermute | solution.py:172
  40.3 0.6 %fusion.5 = s32[]{:T(128)} fusion(s32[16]{0:T(128)S(1)} %reduce, f32[16]{0:T(128)S(1)} %slice_reduce_fusion), kind=kLoop, calls=%fused_computation.35 | loop fusion | flops 591 | bytes 132 | tf_op jit(solution)/shard_map/reduce_max | solution.py:208
  41.7 0.2 collective-permute-done.15
  42.0 1.5 %collective-permute-done.14 = f32[16,256]{1,0:T(8,128)S(1)} collective-permute-done((f32[16,256]{1,0:T(8,128)S(1)}, f32[16,256]{1,0:T(8,128)S(1)}, u32[]{:S(2)}, u32[]{:S(2)}) %collective-permute-start.14) | collective-permute-done | bytes 16416 | tf_op jit(solution)/shard_map/ppermute | solution.py:172
  43.5 0.6 %broadcast_maximum_fusion = f32[256]{0:T(256)} fusion(f32[256]{0:T(256)S(1)} %get-tuple-element.340), kind=kLoop, calls=%fused_computation.37 | loop fusion | flops 256 | bytes 2048 | tf_op jit(solution)/shard_map/max | solution.py:247
  (48 shorter events, 1.0 us)
Async XLA Ops:
  0.0 12.5 %copy-start.3 = (s32[384]{0:T(512)S(1)}, s32[384]{0:T(512)}, u32[]{:S(2)}) copy-start(s32[384]{0:T(512)} %param.12) | copy-start | bytes 4612
  1.3 11.2 %copy-start.4 = (s32[384]{0:T(512)S(1)}, s32[384]{0:T(512)}, u32[]{:S(2)}) copy-start(s32[384]{0:T(512)} %param.13) | copy-start | bytes 4612
  1.3 15.6 %collective-permute-start.7 = (bf16[272,1024]{1,0:T(8,128)(2,1)S(1)}, bf16[272,1024]{1,0:T(8,128)(2,1)S(1)}, u32[]{:S(2)}, u32[]{:S(2)}) collective-permute-start(bf16[272,1024]{1,0:T(8,128)(2,1)S(1)} %shard_map.56.refs_0_.refs_3_.refs_1_), channel_id=1, source_target_pairs={{0,2},{1,3},{2,0},{3,1},{4,6},{5,7},{6,4},{7,5},{8,10},{9,11},{10,... | collective-permute-start | bytes 1671176 | tf_op jit(solution)/shard_map/ppermute | solution.py:172
  4.3 14.2 %collective-permute-start.8 = (bf16[272,1024]{1,0:T(8,128)(2,1)S(1)}, bf16[272,1024]{1,0:T(8,128)(2,1)}, u32[]{:S(2)}, u32[]{:S(2)}) collective-permute-start(bf16[272,1024]{1,0:T(8,128)(2,1)S(1)} %shard_map.56.refs_0_.refs_3_.refs_1_), channel_id=1, source_target_pairs={{0,4},{1,5},{2,6},{3,7},{4,0},{5,1},{6,2},{7,3},{8,12},{9,13},{10,... | collective-permute-start | bytes 1671176 | tf_op jit(solution)/shard_map/ppermute | solution.py:172
  5.8 15.9 %collective-permute-start.9 = (bf16[272,1024]{1,0:T(8,128)(2,1)S(1)}, bf16[272,1024]{1,0:T(8,128)(2,1)S(1)}, u32[]{:S(2)}, u32[]{:S(2)}) collective-permute-start(bf16[272,1024]{1,0:T(8,128)(2,1)S(1)} %shard_map.56.refs_0_.refs_3_.refs_1_), channel_id=1, source_target_pairs={{8,0},{9,1},{10,2},{11,3},{12,4},{13,5},{14,6},{15,7},{16,8},{17,9... | collective-permute-start | bytes 1671176 | tf_op jit(solution)/shard_map/ppermute | solution.py:175
  7.1 15.7 %collective-permute-start.11 = (bf16[272,1024]{1,0:T(8,128)(2,1)S(1)}, bf16[272,1024]{1,0:T(8,128)(2,1)}, u32[]{:S(2)}, u32[]{:S(2)}) collective-permute-start(bf16[272,1024]{1,0:T(8,128)(2,1)S(1)} %shard_map.56.refs_0_.refs_3_.refs_1_), channel_id=1, source_target_pairs={{0,8},{1,9},{2,10},{3,11},{4,12},{5,13},{6,14},{7,15},{8,16},{9,17... | collective-permute-start | bytes 1671176 | tf_op jit(solution)/shard_map/ppermute | solution.py:178
  12.5 10.3 %collective-permute-start.13 = (bf16[272,1024]{1,0:T(8,128)(2,1)S(1)}, bf16[272,1024]{1,0:T(8,128)(2,1)S(1)}, u32[]{:S(2)}, u32[]{:S(2)}) collective-permute-start(bf16[272,1024]{1,0:T(8,128)(2,1)S(1)} %shard_map.56.refs_0_.refs_3_.refs_1_), channel_id=1, source_target_pairs={{0,1},{1,0},{2,3},{3,2},{4,5},{5,4},{6,7},{7,6},{8,9},{9,8},{10,11... | collective-permute-start | bytes 1671176 | tf_op jit(solution)/shard_map/ppermute | solution.py:172
  12.5 0.7 %copy-start = (s32[256]{0:T(256)S(1)}, s32[256]{0:T(256)}, u32[]{:S(2)}) copy-start(s32[256]{0:T(256)} %param.10) | copy-start | bytes 3076
  12.5 0.7 %copy-start.1 = (s32[32]{0:T(128)S(1)}, s32[32]{0:T(128)}, u32[]{:S(2)}) copy-start(s32[32]{0:T(128)} %param.11) | copy-start | bytes 388
  14.0 18.5 %all-to-all-start = ((f32[32,1,128]{2,1,0:T(1,128)}), f32[32,1,128]{2,1,0:T(1,128)S(1)}, u32[]{:S(2)}, u32[]{:S(2)}) async-start(f32[32,1,128]{2,1,0:T(1,128)} %shard_map.55), calls=%async_computation | async-start | bytes 32768 | tf_op jit(solution)/shard_map/all_to_all | solution.py:195
  16.9 12.5 %copy-start.2 = (bf16[272,1024]{1,0:T(8,128)(2,1)}, bf16[272,1024]{1,0:T(8,128)(2,1)S(1)}, u32[]{:S(2)}) copy-start(bf16[272,1024]{1,0:T(8,128)(2,1)S(1)} %collective-permute-done.7.x_ref.refs_1_) | copy-start | bytes 1671172
  19.6 7.0 %collective-permute-start.16 = (bf16[128,1024]{1,0:T(8,128)(2,1)S(1)}, bf16[128,1024]{1,0:T(8,128)(2,1)S(1)}, u32[]{:S(2)}, u32[]{:S(2)}) collective-permute-start(bf16[128,1024]{1,0:T(8,128)(2,1)S(1)} %get-tuple-element.180), channel_id=1, source_target_pairs={{0,4},{1,5},{2,6},{3,7},{4,0},{5,1},{6,2},{7,3},{8,12},{9,13},{10,... | collective-permute-start | bytes 786440 | tf_op jit(solution)/shard_map/ppermute | solution.py:172
  21.2 7.4 %collective-permute-start.17 = (bf16[144,1024]{1,0:T(8,128)(2,1)S(1)}, bf16[144,1024]{1,0:T(8,128)(2,1)S(1)}, u32[]{:S(2)}, u32[]{:S(2)}) collective-permute-start(bf16[144,1024]{1,0:T(8,128)(2,1)S(1)} %get-tuple-element.190), channel_id=1, source_target_pairs={{0,2},{1,3},{2,0},{3,1},{4,6},{5,7},{6,4},{7,5},{8,10},{9,11},{10,... | collective-permute-start | bytes 884744 | tf_op jit(solution)/shard_map/ppermute | solution.py:172
  21.7 12.7 %copy-start.5 = (bf16[272,1024]{1,0:T(8,128)(2,1)}, bf16[272,1024]{1,0:T(8,128)(2,1)S(1)}, u32[]{:S(2)}) copy-start(bf16[272,1024]{1,0:T(8,128)(2,1)S(1)} %collective-permute-done.9.refs_3_) | copy-start | bytes 1671172
  21.7 7.7 %collective-permute-start.10 = (bf16[272,1024]{1,0:T(8,128)(2,1)S(1)}, bf16[272,1024]{1,0:T(8,128)(2,1)S(1)}, u32[]{:S(2)}, u32[]{:S(2)}) collective-permute-start(bf16[272,1024]{1,0:T(8,128)(2,1)S(1)} %collective-permute-done.9.refs_3_), channel_id=1, source_target_pairs={{0,1},{1,0},{2,3},{3,2},{4,5},{5,4},{6,7},{7,6},{8,9},{9,8},{10,11... | collective-permute-start | bytes 1671176 | tf_op jit(solution)/shard_map/ppermute | solution.py:172
  22.8 6.6 %collective-permute-start.12 = (bf16[272,1024]{1,0:T(8,128)(2,1)}, bf16[272,1024]{1,0:T(8,128)(2,1)S(1)}, u32[]{:S(2)}, u32[]{:S(2)}) collective-permute-start(bf16[272,1024]{1,0:T(8,128)(2,1)} %collective-permute-done.11.refs_5_), channel_id=1, source_target_pairs={{0,1},{1,0},{2,3},{3,2},{4,5},{5,4},{6,7},{7,6},{8,9},{9,8},{10,11... | collective-permute-start | bytes 1671176 | tf_op jit(solution)/shard_map/ppermute | solution.py:172
  36.7 6.8 %copy-start.6 = (bf16[272,1024]{1,0:T(8,128)(2,1)S(1)}, bf16[272,1024]{1,0:T(8,128)(2,1)}, u32[]{:S(2)}) copy-start(bf16[272,1024]{1,0:T(8,128)(2,1)} %copy-done.5) | copy-start | bytes 1671172
  36.7 5.0 %collective-permute-start.18 = (f32[16,256]{1,0:T(8,128)S(1)}, f32[16,256]{1,0:T(8,128)S(1)}, u32[]{:S(2)}, u32[]{:S(2)}) collective-permute-start(f32[16,256]{1,0:T(8,128)S(1)} %shard_map.61), channel_id=1, source_target_pairs={{0,6},{1,7},{2,4},{3,5},{4,2},{5,3},{6,0},{7,1},{8,14},{9,15},{10,... | collective-permute-start | bytes 49160 | tf_op jit(solution)/shard_map/ppermute | solution.py:172
  38.2 3.7 %collective-permute-start.15 = (f32[16,256]{1,0:T(8,128)S(1)}, f32[16,256]{1,0:T(8,128)S(1)}, u32[]{:S(2)}, u32[]{:S(2)}) collective-permute-start(f32[16,256]{1,0:T(8,128)S(1)} %get-tuple-element.189), channel_id=1, source_target_pairs={{0,4},{1,5},{2,6},{3,7},{4,0},{5,1},{6,2},{7,3},{8,12},{9,13},{10,... | collective-permute-start | bytes 49160 | tf_op jit(solution)/shard_map/ppermute | solution.py:172
  39.7 3.7 %collective-permute-start.14 = (f32[16,256]{1,0:T(8,128)S(1)}, f32[16,256]{1,0:T(8,128)S(1)}, u32[]{:S(2)}, u32[]{:S(2)}) collective-permute-start(f32[16,256]{1,0:T(8,128)S(1)} %get-tuple-element.188), channel_id=1, source_target_pairs={{0,2},{1,3},{2,0},{3,1},{4,6},{5,7},{6,4},{7,5},{8,10},{9,11},{10,... | collective-permute-start | bytes 49160 | tf_op jit(solution)/shard_map/ppermute | solution.py:172
